TPU v7x, 128 devices: a whole 4x4x4 slice. The times are simulated.
128 devices in a mesh: row: 8 (over x, y_lo), col: 16 (over y_hi, z, core).
Axes of the slice: x: 4, y: 4 (y_hi: 2, y_lo: 2; y = y_hi * 2 + y_lo), z: 4, core: 2. Of those that a mesh axis runs over, the one named last changes fastest.
Arguments:
- homolog_tensor: float32 [512, 512, 256], P('row', 'col'), may hold values from -6 to 6
- couplings: float32 [512, 512, 128], P('row', 'col'), may hold values from -6 to 6
- attention_probe_matrix: bfloat16 [256, 256], replicated, may hold values from -4 to 4
- attention_extra_matrices: bfloat16 [256, 768], replicated, may hold values from -0.375 to 0.375
- attention_final_matrix: bfloat16 [256, 256], replicated, may hold values from -0.375 to 0.375
- tensor_entry_matrices: bfloat16 [256, 64], replicated, may hold values from -0.375 to 0.375
- tensor_final_matrix: bfloat16 [1024, 128], replicated, may hold values from -4 to 4
- incoming_entry_matrices: bfloat16 [128, 512], replicated, may hold values from -0.5 to 0.5
- incoming_switch_matrix: bfloat16 [128, 128], replicated, may hold values from -0.5 to 0.5
- incoming_final_matrix: bfloat16 [128, 128], replicated, may hold values from -0.5 to 0.5
Outputs:
- refreshed_homologs: float32 [512, 512, 256], P('row', 'col')
- pair_output: float32 [512, 512, 128], P('row', 'col')
All inputs are finite; a program needn't handle non-finite values.
Results may differ from a plain program's by a relative error of at most 0.017.
The roundings to bfloat16 on the way count: a program that leaves them out, or rounds other values in their place, can miss the bound.
Values may be sent and summed in bfloat16 or wider, within the bound.
A program may use at most 128 MiB of HBM per device.

v0:
```python
import jax
import jax.numpy as jnp
from jax import lax
from jax.sharding import PartitionSpec as P

FEATURE_DEPTH = 256
C_Z = 128
TENSOR_FEATURES = 32
C_TRI = 128
ATTENTION_UNITS = 8
UNIT_WIDTH = 32


def broadcast(block, axis, owner):
    block = jnp.where(lax.axis_index(axis) == owner, block, jnp.zeros_like(block))
    return lax.psum(block, axis)


def standardise_features(attended_contents):
    centre = jnp.mean(attended_contents, axis=-1, keepdims=True)
    centred = attended_contents - centre
    spread = jnp.mean(centred * centred, axis=-1, keepdims=True)
    return centred * lax.rsqrt(spread + 1e-05)


def attend_column(column, attention_probe_matrix, attention_extra_matrices):
    homolog_amount = column.shape[0]
    inner_width = ATTENTION_UNITS * UNIT_WIDTH
    queries = (
        jnp.dot(column, attention_probe_matrix, preferred_element_type=jnp.float32)
        * UNIT_WIDTH ** (-0.5)
    ).astype(jnp.bfloat16)
    projected_rows = jnp.dot(column, attention_extra_matrices, preferred_element_type=jnp.float32)
    key_rows = projected_rows[:, :inner_width].astype(jnp.bfloat16)
    value_rows = projected_rows[:, inner_width : 2 * inner_width].astype(jnp.bfloat16)
    gate_cols = jax.nn.sigmoid(projected_rows[:, 2 * inner_width :])
    queries = queries.reshape(homolog_amount, ATTENTION_UNITS, UNIT_WIDTH)
    key_rows = key_rows.reshape(homolog_amount, ATTENTION_UNITS, UNIT_WIDTH)
    value_rows = value_rows.reshape(homolog_amount, ATTENTION_UNITS, UNIT_WIDTH)
    scores = jnp.einsum("shd,thd->hst", queries, key_rows, preferred_element_type=jnp.float32)
    weights = jax.nn.softmax(scores, axis=-1).astype(jnp.bfloat16)
    attended = jnp.einsum("hst,thd->shd", weights, value_rows, preferred_element_type=jnp.float32)
    attended = attended.reshape(homolog_amount, inner_width)
    return (attended * gate_cols).astype(jnp.bfloat16)


def route_alignment(left_piece, right_piece):
    group_ratio = lax.axis_size("col") // lax.axis_size("row")
    left_rows, right_gathered = (
        lax.all_gather(left_piece, "row", axis=0, tiled=True),
        lax.all_gather(right_piece, "row", axis=0, tiled=True),
    )
    pieces = []
    for offset in range(group_ratio):
        pieces.append(broadcast(left_rows, "col", group_ratio * lax.axis_index("row") + offset))
    left_gathered = jnp.concatenate(pieces, axis=1)
    return (left_gathered, right_gathered)


def route_pair(left_piece, right_piece):
    group_ratio = lax.axis_size("col") // lax.axis_size("row")
    left_rows, right_gathered = (
        lax.all_gather(left_piece, "row", axis=0, tiled=True),
        lax.all_gather(right_piece, "row", axis=0, tiled=True),
    )
    pieces = []
    for offset in range(group_ratio):
        pieces.append(broadcast(left_rows, "col", group_ratio * lax.axis_index("row") + offset))
    left_gathered = jnp.concatenate(pieces, axis=1)
    return (left_gathered, right_gathered)


def body(
    homolog_tensor,
    couplings,
    attention_probe_matrix,
    attention_extra_matrices,
    attention_final_matrix,
    tensor_entry_matrices,
    tensor_final_matrix,
    incoming_entry_matrices,
    incoming_switch_matrix,
    incoming_final_matrix,
):
    homolog_lines = homolog_tensor.shape[0]
    amino_positions = homolog_tensor.shape[1]
    standardised = standardise_features(homolog_tensor).astype(jnp.bfloat16)
    by_residue = lax.all_to_all(standardised, "row", split_axis=1, concat_axis=0, tiled=True)
    attended = lax.map(
        lambda column: attend_column(column, attention_probe_matrix, attention_extra_matrices),
        jnp.transpose(by_residue, (1, 0, 2)),
    )
    gated = lax.all_to_all(
        jnp.transpose(attended, (1, 0, 2)), "row", split_axis=0, concat_axis=1, tiled=True
    )
    residual_change = jnp.dot(
        gated.reshape(-1, ATTENTION_UNITS * UNIT_WIDTH),
        attention_final_matrix,
        preferred_element_type=jnp.float32,
    )
    refreshed_homologs = homolog_tensor + residual_change.reshape(homolog_tensor.shape)
    standardised_result = (
        standardise_features(refreshed_homologs).astype(jnp.bfloat16).reshape(-1, FEATURE_DEPTH)
    )
    projected_rows = jnp.dot(
        standardised_result, tensor_entry_matrices, preferred_element_type=jnp.float32
    ).astype(jnp.bfloat16)
    projected_rows = projected_rows.reshape(homolog_lines, amino_positions, 2 * TENSOR_FEATURES)
    left_piece = projected_rows[:, :, :TENSOR_FEATURES].reshape(
        homolog_lines, amino_positions * TENSOR_FEATURES
    )
    right_piece = projected_rows[:, :, TENSOR_FEATURES:].reshape(
        homolog_lines, amino_positions * TENSOR_FEATURES
    )
    left_gathered, right_gathered = route_alignment(left_piece, right_piece)
    total_seqs = left_gathered.shape[0]
    row_res = left_gathered.shape[1] // TENSOR_FEATURES
    outer_product_sum = lax.dot_general(
        left_gathered, right_gathered, (((0,), (0,)), ((), ())), preferred_element_type=jnp.float32
    )
    outer_product_sum = outer_product_sum.reshape(
        row_res, TENSOR_FEATURES, amino_positions, TENSOR_FEATURES
    )
    outer_product_sum = jnp.transpose(outer_product_sum, (0, 2, 1, 3)).reshape(
        row_res * amino_positions, TENSOR_FEATURES * TENSOR_FEATURES
    )
    outer_mean = (outer_product_sum / total_seqs).astype(jnp.bfloat16)
    opm_update = jnp.dot(outer_mean, tensor_final_matrix, preferred_element_type=jnp.float32)
    pair_mid = couplings + opm_update.reshape(couplings.shape)
    pair_rows = couplings.shape[0]
    pair_normed = standardise_features(pair_mid).astype(jnp.bfloat16).reshape(-1, C_Z)
    projected_rows = jnp.dot(
        pair_normed, incoming_entry_matrices, preferred_element_type=jnp.float32
    )
    left_pair = (
        jax.nn.sigmoid(projected_rows[:, C_TRI : 2 * C_TRI]) * projected_rows[:, :C_TRI]
    ).astype(jnp.bfloat16)
    right_pair = (
        jax.nn.sigmoid(projected_rows[:, 3 * C_TRI :]) * projected_rows[:, 2 * C_TRI : 3 * C_TRI]
    ).astype(jnp.bfloat16)
    gate_pair = jax.nn.sigmoid(
        jnp.dot(pair_normed, incoming_switch_matrix, preferred_element_type=jnp.float32)
    )
    left_gathered, right_gathered = route_pair(
        left_pair.reshape(pair_rows, amino_positions * C_TRI),
        right_pair.reshape(pair_rows, amino_positions * C_TRI),
    )
    k_count = left_gathered.shape[0]
    product = jnp.einsum(
        "kic,kjc->ijc",
        left_gathered.reshape(k_count, -1, C_TRI),
        right_gathered.reshape(k_count, -1, C_TRI),
        preferred_element_type=jnp.float32,
    )
    product_normed = standardise_features(product).astype(jnp.bfloat16).reshape(-1, C_TRI)
    tri_update = jnp.dot(product_normed, incoming_final_matrix, preferred_element_type=jnp.float32)
    pair_output = pair_mid + (gate_pair * tri_update).reshape(couplings.shape)
    return (refreshed_homologs, pair_output)


def solution(mesh):
    in_specs = (
        P("row", "col", None),
        P("row", "col", None),
        P(),
        P(),
        P(),
        P(),
        P(),
        P(),
        P(),
        P(),
    )
    out_specs = (P("row", "col", None), P("row", "col", None))
    return jax.shard_map(body, mesh=mesh, in_specs=in_specs, out_specs=out_specs, check_vma=False)
```

profile of v0, /device:TPU:1, one launch (start us, length us, event | category | flops | bytes accessed | tf_op | source)
XLA Modules:
  0.0 791.8 jit_solution(10611434739273157062)
XLA Ops:
  9.4 3.1 multiply_reduce_fusion.2
  14.7 5.9 all-to-all-start
  20.6 15.1 %all-to-all-done = bf16[64,32,256]{2,0,1:T(8,128)(2,1)S(1)} async-done(((bf16[64,32,256]{2,0,1:T(8,128)(2,1)}), bf16[64,32,256]{2,0,1:T(8,128)(2,1)S(1)}, u32[]{:S(2)}, u32[]{:S(2)}) %all-to-all-start) | async-done | bytes 1048608 | tf_op jit(solution)/shard_map/all_to_all | solution.py:88
  36.8 42.3 %while.10 = (s32[]{:T(128)}, bf16[4,512,256]{2,1,0:T(8,128)(2,1)}, bf16[4,512,256]{2,1,0:T(8,128)(2,1)}, bf16[256,768]{1,0:T(8,128)(2,1)S(1)}, bf16[256,256]{1,0:T(8,128)(2,1)}, /*index=5*/s32[]{:T(128)}) while((s32[]{:T(128)}, bf16[4,512,256]{2,1,0:T(8,128)(2,1)}, bf16[4,512,256]{2,1,0:T(8,128)(2,1)}, bf16[256,768]{1,0:T(8,128)(2,1)S(1)}, ...), condition=%wide.region_5.6_spmd, body=%wide.region_2.5_spmd.sunk | while | flops 682890240 | bytes 11042933 | solution.py:89
  43.0 3.3 fusion.94
  53.5 3.3 fusion.94
  64.1 3.3 fusion.94
  74.7 3.3 fusion.94
  81.3 27.1 %all_to_all.33 = bf16[512,4,256]{2,1,0:T(4,128)(2,1)S(1)} all-to-all(bf16[512,4,256]{2,1,0:T(4,128)(2,1)S(1)} %bitcast.116), channel_id=1, replica_groups=mesh['row'=8,'col'=16] {'row'}, dimensions={0} | all-to-all | bytes 2097152 | tf_op jit(solution)/shard_map/all_to_all | solution.py:93
  121.5 35.7 %all-gather.5.cloned.1.call-done = bf16[512,1024]{1,0:T(8,128)(2,1)} async-done(((bf16[64,1024]{1,0:T(8,128)(2,1)}), bf16[512,1024]{1,0:T(8,128)(2,1)}) %all-gather.5.cloned.1.call-update) | async-done | bytes 1048592 | tf_op jit(solution)/shard_map/all_gather | solution.py:50
  159.9 37.4 %all-gather.7.cloned.1.call-done = bf16[512,1024]{1,0:T(8,128)(2,1)} async-done(((bf16[64,1024]{1,0:T(8,128)(2,1)}), bf16[512,1024]{1,0:T(8,128)(2,1)}) %all-gather.7.cloned.1.call-update) | async-done | bytes 1048592 | tf_op jit(solution)/shard_map/all_gather | solution.py:51
  197.3 151.4 %all-reduce.7.cloned.1.call-done = (bf16[512,1024]{1,0:T(8,128)(2,1)}, bf16[512,1024]{1,0:T(8,128)(2,1)}) async-done(((bf16[512,1024]{1,0:T(8,128)(2,1)}, bf16[512,1024]{1,0:T(8,128)(2,1)}), (bf16[512,1024]{1,0:T(8,128)(2,1)}, bf16[512,1024]{1,0:T(8,128)(2,1)})) %all-reduce.7.cloned.1.call-update) | async-done | bytes 2097168 | tf_op jit(solution)/shard_map/psum | solution.py:16
  348.7 6.2 multiply_convert_fusion
  354.9 20.3 %convert_element_type.49 = bf16[64,32,32,32]{3,2,1,0:T(8,128)(2,1)} reshape(bf16[2048,1024]{1,0:T(8,128)(2,1)} %multiply_convert_fusion) | data formatting | bytes 8388608 | tf_op jit(solution)/shard_map/convert_element_type | solution.py:127
  375.2 21.8 %copy.178 = bf16[64,32,32,32]{0,3,2,1:T(8,128)(2,1)} copy(bf16[64,32,32,32]{3,1,2,0:T(8,128)(2,1)} %bitcast.102) | data formatting | bytes 8388608 | tf_op jit(solution)/shard_map/convert_element_type | solution.py:127
  397.0 6.3 fusion.47
  408.4 89.9 %all-gather.11.cloned.1.call-done = bf16[512,4096]{1,0:T(8,128)(2,1)} async-done(((bf16[64,4096]{1,0:T(8,128)(2,1)}), bf16[512,4096]{1,0:T(8,128)(2,1)}) %all-gather.11.cloned.1.call-update) | async-done | bytes 4194320 | tf_op jit(solution)/shard_map/all_gather | solution.py:63
  498.2 6.5 copy.183
  504.7 6.1 broadcast_select_fusion.1
  513.0 79.0 %all-gather.9.cloned.1.call-done = bf16[512,4096]{1,0:T(8,128)(2,1)} async-done(((bf16[64,4096]{1,0:T(8,128)(2,1)}), bf16[512,4096]{1,0:T(8,128)(2,1)}) %all-gather.9.cloned.1.call-update) | async-done | bytes 4194320 | tf_op jit(solution)/shard_map/all_gather | solution.py:64
  592.0 6.5 copy.182
  598.5 161.5 %all-reduce.5.cloned.1.call-done = (bf16[512,4096]{0,1:T(8,128)(2,1)}, bf16[512,4096]{0,1:T(8,128)(2,1)}) async-done(((bf16[512,4096]{0,1:T(8,128)(2,1)}, bf16[512,4096]{0,1:T(8,128)(2,1)}), (bf16[512,4096]{0,1:T(8,128)(2,1)}, bf16[512,4096]{0,1:T(8,128)(2,1)})) %all-reduce.5.cloned.1.call-update) | async-done | bytes 8388624 | tf_op jit(solution)/shard_map/psum | solution.py:16
  760.0 7.2 pad_maximum_fusion
  767.2 11.4 %bitcast_reduce_fusion = (f32[64,32]{0,1:T(8,128)S(1)}, f32[128,32,64]{2,1,0:T(8,128)S(1)}) fusion(bf16[512,64,128]{0,2,1:T(8,128)(2,1)} %bitcast.105, bf16[512,32,128]{0,2,1:T(8,128)(2,1)} %bitcast.113), kind=kOutput, calls=%fused_computation.39 | convolution fusion | flops 268695552 | bytes 13639680 | tf_op jit(solution)/shard_map/kic,kjc->ijc/dot_general | solution.py:149
  (117 shorter events, 65.2 us)
Async XLA Ops:
  7.2 389.8 %copy-start = (bf16[1024,128]{1,0:T(8,128)(2,1)S(1)}, bf16[1024,128]{1,0:T(8,128)(2,1)}, u32[]{:S(2)}) copy-start(bf16[1024,128]{1,0:T(8,128)(2,1)} %param.18) | copy-start | bytes 786436
  7.2 5.3 copy-start.1
  12.5 24.3 %copy-start.3 = (bf16[256,768]{1,0:T(8,128)(2,1)S(1)}, bf16[256,768]{1,0:T(8,128)(2,1)}, u32[]{:S(2)}) copy-start(bf16[256,768]{1,0:T(8,128)(2,1)} %param.15) | copy-start | bytes 1179652
  14.7 21.0 %all-to-all-start = ((bf16[64,32,256]{2,0,1:T(8,128)(2,1)}), bf16[64,32,256]{2,0,1:T(8,128)(2,1)S(1)}, u32[]{:S(2)}, u32[]{:S(2)}) async-start(bf16[64,32,256]{2,0,1:T(8,128)(2,1)} %multiply_convert_fusion.3), calls=%async_computation | async-start | bytes 2097152 | tf_op jit(solution)/shard_map/all_to_all | solution.py:88
  20.6 136.6 %all-gather.5.cloned.1.call-start = ((), (), s32[]{:S(2)}) async-start(), calls=%async_computation.2 | async-start | bytes 1179648 | tf_op jit(solution)/shard_map/all_gather | solution.py:50
  40.4 2.6 copy-start.4
  51.0 2.6 copy-start.4
  61.5 2.6 copy-start.4
  72.1 2.6 copy-start.4
  79.1 31.0 %copy-start.2 = (f32[64,32,256]{2,1,0:T(8,128)S(1)}, f32[64,32,256]{2,1,0:T(8,128)}, u32[]{:S(2)}) copy-start(f32[64,32,256]{2,1,0:T(8,128)} %param.12) | copy-start | bytes 6291460
  79.1 31.0 %copy-start.7 = (bf16[256,256]{1,0:T(8,128)(2,1)S(1)}, bf16[256,256]{1,0:T(8,128)(2,1)}, u32[]{:S(2)}) copy-start(bf16[256,256]{1,0:T(8,128)(2,1)} %param.16) | copy-start | bytes 393220
  110.1 7.5 copy-start.8
  120.0 77.3 %all-gather.7.cloned.1.call-start = ((), (), s32[]{:S(2)}) async-start(), calls=%async_computation.3 | async-start | bytes 1179648 | tf_op jit(solution)/shard_map/all_gather | solution.py:51
  121.4 227.3 %all-reduce.7.cloned.1.call-start = ((), (), s32[]{:S(2)}) async-start(), calls=%async_computation.7 | async-start | bytes 4194304 | tf_op jit(solution)/shard_map/psum | solution.py:16
  159.9 338.3 %all-gather.11.cloned.1.call-start = ((), (), s32[]{:S(2)}) async-start(), calls=%async_computation.5 | async-start | bytes 4718592 | tf_op jit(solution)/shard_map/all_gather | solution.py:63
  375.2 21.8 %copy-start.5 = (f32[64,32,128]{2,1,0:T(8,128)S(1)}, f32[64,32,128]{2,1,0:T(8,128)}, u32[]{:S(2)}) copy-start(f32[64,32,128]{2,1,0:T(8,128)} %param.13) | copy-start | bytes 3145732
  396.9 8.0 %copy-start.6 = (bf16[128,512]{1,0:T(8,128)(2,1)S(1)}, bf16[128,512]{1,0:T(8,128)(2,1)}, u32[]{:S(2)}) copy-start(bf16[128,512]{1,0:T(8,128)(2,1)} %param.19) | copy-start | bytes 393220
  407.2 184.8 %all-gather.9.cloned.1.call-start = ((), (), s32[]{:S(2)}) async-start(), calls=%async_computation.4 | async-start | bytes 4718592 | tf_op jit(solution)/shard_map/all_gather | solution.py:64
  408.3 351.7 %all-reduce.5.cloned.1.call-start = ((), (), s32[]{:S(2)}) async-start(), calls=%async_computation.6 | async-start | bytes 16777216 | tf_op jit(solution)/shard_map/psum | solution.py:16
  510.8 0.8 copy-start.10
  778.7 2.2 copy-start.9
Sparse Core Ops, SparseCore 0:
  120.1 37.0 all-gather.4
  158.8 38.4 all-gather.6
  200.4 148.2 all-reduce.6
  407.3 90.8 all-gather.10
  499.7 92.2 all-gather.8
  594.4 165.5 all-reduce.4
where the time goes:
time: 801 us; the launch traced here: 792 us
  waiting for transfers between devices  570 us (71%)
  local copies, waits for them, and re-layouts  74.8 us (9%)
  matrix products  64.6 us (8%)
  other arithmetic  34.1 us (4%)
  blocking collectives  27.1 us (3%)
  between operations  14.7 us (2%)
    psum x2, waiting for transfers between devices, broadcast(): return lax.psum(block, axis)  313 us
    all_gather x1, waiting for transfers between devices, route_pair(): lax.all_gather(left_piece, 'row', axis=0, tiled=True)  89.9 us
    all_gather x1, waiting for transfers between devices, route_pair(): lax.all_gather(right_piece, 'row', axis=0, tiled=True)  79 us
    convert_element_type x2, local copies, waits for them, and re-layouts, body(): outer_mean = (outer_product_sum / total_seqs).astype(jnp.bfloat16)  42.1 us
    all_gather x1, waiting for transfers between devices, route_alignment(): lax.all_gather(right_piece, 'row', axis=0, tiled=True)  37.4 us
    all_gather x1, waiting for transfers between devices, route_alignment(): lax.all_gather(left_piece, 'row', axis=0, tiled=True)  35.7 us
    all_to_all x1, blocking collectives, body(): lax.all_to_all(jnp.transpose(attended, (1, 0, 2)), 'row', split_axis=0, c...  27.1 us
  transfers between devices with their start and end apart: 7, of which 7 were waited for; matrix products, arithmetic and copies ran while one was open for 3% of the time, Pallas kernels for 0%

commit v1 on v0

v1 whole, which is shorter than its diff:
```python
import functools

import jax
import jax.numpy as jnp
from jax import lax
from jax.experimental import pallas as pl
from jax.experimental.pallas import tpu as pltpu
from jax.sharding import PartitionSpec as P

F32, BF16 = jnp.float32, jnp.bfloat16
MESH = pl.DeviceIdType.MESH
EPS = 1e-05
ROWS, COLS = 8, 16
DEVICES = ROWS * COLS
SEQ, RES = 64, 32
OWN = 4
ALL = 512
FEAT, HEADS = 256, 8
C_Z = 128


def dot(a, b):
    return jnp.dot(a, b, preferred_element_type=F32)


def dot_nt(a, b):
    return lax.dot_general(a, b, (((1,), (1,)), ((), ())), preferred_element_type=F32)


def dot_tn(a, b):
    return lax.dot_general(a, b, (((0,), (0,)), ((), ())), preferred_element_type=F32)


def lane(width):
    return lax.broadcasted_iota(jnp.int32, (1, width), 1)


def head_mask(width, which):
    return jnp.where((lane(width) >> 5) == which, 1.0, 0.0).astype(BF16)


def kernel(
    x_ref, coup_ref, wq_ref, wx_ref, wf_ref, we_ref, wo_ref, wi_ref, wsw_ref, wtri_ref,
    out_m, out_p,
    xs, nt, g, sig, sg, qs, kt, vs, ga, gt, gb, lrs, rb, lb,
    wet, wit, wof, wbd, perm, rf, rp, om, pm, gp, cf, cb, xlr, am, bm, pb, xe, es, er, ef,
    s_x, s_a, r_a, s_sig, r_sig, s_b, r_b, s_l, r_l, s_r, r_r, s_d, r_d, s_e, r_e,
):
    r = lax.axis_index("row")
    c = lax.axis_index("col")
    me = r * COLS + c
    rho = c // 2

    def remote(src, dst, send, recv, row, col):
        return pltpu.make_async_remote_copy(
            src_ref=src, dst_ref=dst, send_sem=send, recv_sem=recv,
            device_id=(row, col), device_id_type=MESH,
        )

    def arrived(ref, sem):
        pltpu.make_async_copy(ref, ref, sem).wait()

    load = [
        pltpu.make_async_copy(x_ref.at[:, pl.ds(k * 128, 128)], xs.at[k], s_x.at[k])
        for k in range(2)
    ]
    load[0].start()
    load[1].start()

    barrier = pltpu.get_barrier_semaphore()

    def greet(d, carry):
        peer = lax.rem(me + d, DEVICES)
        pl.semaphore_signal(
            barrier, inc=1, device_id=(peer // COLS, lax.rem(peer, COLS)), device_id_type=MESH
        )
        return carry

    lax.fori_loop(1, DEVICES, greet, 0)

    def norm_one(q, row, stats):
        n = row * OWN + q
        x0 = xs[0, pl.ds(n, SEQ, stride=RES), :]
        x1 = xs[1, pl.ds(n, SEQ, stride=RES), :]
        mean = jnp.sum(x0 + x1, axis=-1, keepdims=True) * (1.0 / FEAT)
        x0, x1 = x0 - mean, x1 - mean
        var = jnp.sum(x0 * x0 + x1 * x1, axis=-1, keepdims=True) * (1.0 / FEAT) + EPS
        inv = lax.rsqrt(var)
        nt[q, row, :, 0:128] = (x0 * inv).astype(BF16)
        nt[q, row, :, 128:256] = (x1 * inv).astype(BF16)
        sd = var * inv
        high = sd.astype(BF16).astype(F32)
        stats = jnp.where(lane(128) == n, high, stats)
        return jnp.where(lane(128) == n + RES, sd - high, stats)

    load[0].wait()
    load[1].wait()
    stats = jnp.zeros((SEQ, 128), F32)
    for q in range(OWN):
        stats = lax.fori_loop(0, ROWS, lambda row, s, q=q: norm_one(q, row, s), stats)
        if q == 0:
            pl.semaphore_wait(barrier, DEVICES - 1)

        def send_a(j, carry, q=q):
            row = lax.rem(r + j, ROWS)
            remote(nt.at[q, row], g.at[q, r], s_a.at[q], r_a.at[q], row, c).start()
            return carry

        lax.fori_loop(1, ROWS, send_a, 0)
        pltpu.make_async_copy(nt.at[q, r], g.at[q, r], r_a.at[q]).start()
    sig[...] = stats.astype(BF16)

    def send_sig(j, carry):
        row = lax.rem(r + j, ROWS)
        remote(sig, sg.at[r], s_sig, r_sig, row, c).start()
        return carry

    lax.fori_loop(1, ROWS, send_sig, 0)
    pltpu.make_async_copy(sig, sg.at[r], r_sig).start()

    wet[...] = we_ref[...].astype(F32).T.astype(BF16)
    wit[...] = wi_ref[...].astype(F32).T.astype(BF16)
    wof[...] = wo_ref[...].astype(F32)
    wbd[...] = jnp.zeros(wbd.shape, BF16)

    def spread(d, carry):
        block = wof[pl.ds(d, 32, stride=32), :].astype(BF16)
        for a in range(4):
            at = pl.multiple_of(d * 128 + a * 32, 32)
            wbd[pl.ds(at, 32), a * 128 : (a + 1) * 128] = block
        return carry

    lax.fori_loop(0, 32, spread, 0)
    source = lax.broadcasted_iota(jnp.int32, (512, 512), 0)
    target = ((source >> 5) & 3) * 128 + (source >> 7) * 32 + (source & 31)
    column = lax.broadcasted_iota(jnp.int32, (512, 512), 1)
    perm[...] = jnp.where(column == target, 1.0, 0.0).astype(BF16)

    def attend(q, carry):
        arrived(g.at[q], r_a.at[q])
        column = g[q].reshape(ALL, FEAT)
        qs[...] = (dot(column, wq_ref[...]) * 32 ** (-0.5)).astype(BF16)
        kt[...] = dot(column, wx_ref[:, 0:256]).T.astype(BF16)
        vs[...] = dot(column, wx_ref[:, 256:512]).astype(BF16)
        ga[...] = jax.nn.sigmoid(dot(column, wx_ref[:, 512:768]))
        for tile in range(2):
            cols = slice(tile * 128, tile * 128 + 128)
            for part in range(2):
                rows = slice(part * 256, part * 256 + 256)
                top = jnp.zeros((256, 128), F32)
                low = jnp.ones((256, 128), F32)
                for h in range(4):
                    mask = head_mask(128, h)
                    values = vs[:, cols] * mask + (1 - mask)
                    scores = dot(qs[rows, :] * head_mask(256, tile * 4 + h), kt[...])
                    best = jnp.max(scores, axis=-1, keepdims=True)
                    weights = jnp.exp(scores - best).astype(BF16)
                    found = dot(weights, values)
                    here = (lane(128) >> 5) == h
                    top = jnp.where(here, found, top)
                    low = jnp.where(here, pltpu.roll(found, 32, 1), low)
                gated = (top / low * ga[rows, cols]).astype(BF16)
                gt[q, part * 4 : part * 4 + 4, :, cols] = gated.reshape(4, SEQ, 128)

        def send_b(j, carry):
            row = lax.rem(r + j, ROWS)
            remote(gt.at[q, row], gb.at[r * OWN + q], s_b, r_b, row, c).start()
            return carry

        @pl.when(q == 0)
        def _():
            arrived(sg, r_sig)

        for part in range(2):
            rows = slice(part * 256, part * 256 + 256)
            gated = gt[q, part * 4 : part * 4 + 4].reshape(256, FEAT)
            normed = g[q, part * 4 : part * 4 + 4].reshape(256, FEAT).astype(F32)
            spreads = sg[part * 4 : part * 4 + 4].reshape(256, 128).astype(F32)
            n = r * OWN + q
            here = jnp.logical_or(lane(128) == n, lane(128) == n + RES)
            sd = jnp.sum(jnp.where(here, spreads, 0.0), axis=-1, keepdims=True)
            fresh = normed + dot(gated, wf_ref[...]) * (1.0 / sd)
            fresh = fresh - jnp.mean(fresh, axis=-1, keepdims=True)
            var = jnp.mean(fresh * fresh, axis=-1, keepdims=True)
            fresh = (fresh * (sd * lax.rsqrt(sd * sd * var + EPS))).astype(BF16)
            lrs[q, :, rows] = dot_nt(wet[...], fresh).astype(BF16)

        def send_r(j, carry):
            row = lax.rem(r + j, ROWS)
            remote(lrs.at[q, pl.ds(32, 32)], rb.at[r * OWN + q], s_r, r_r, row, c).start()
            return carry

        lax.fori_loop(1, ROWS, send_r, 0)
        pltpu.make_async_copy(lrs.at[q, pl.ds(32, 32)], rb.at[r * OWN + q], r_r).start()
        spot = lax.rem(c, 2) * RES + r * OWN + q

        def send_l(j, carry):
            col = lax.rem(c + j, COLS)
            remote(lrs.at[q, pl.ds(0, 32)], lb.at[spot], s_l, r_l, rho, col).start()
            return carry

        lax.fori_loop(1, COLS, send_l, 0)

        @pl.when(rho == r)
        def _():
            pltpu.make_async_copy(lrs.at[q, pl.ds(0, 32)], lb.at[spot], r_l).start()

        @pl.when(rho != r)
        def _():
            remote(lrs.at[q, pl.ds(0, 32)], lb.at[spot], s_l, r_l, rho, c).start()

        lax.fori_loop(1, ROWS, send_b, 0)
        pltpu.make_async_copy(gt.at[q, r], gb.at[r * OWN + q], r_b).start()
        return carry

    lax.fori_loop(0, OWN, attend, 0)

    arrived(rb, r_r)
    for k in range(4):
        rf[k] = rb[:, :, k * 128 : k * 128 + 128].astype(F32).reshape(1024, 128)

    def by_channel(d, carry):
        at = pl.multiple_of(d * 32, 32)
        for k in range(4):
            rp[pl.ds(at, 32), k * 128 : k * 128 + 128] = rf[
                k, pl.ds(d, 32, stride=32), :
            ].astype(BF16)
        return carry

    lax.fori_loop(0, 32, by_channel, 0)

    arrived(lb, r_l)

    def outer(b, carry):
        left = lb[pl.ds(b * 8, 8)].reshape(256, ALL)
        for d in range(0, 32, 8):
            block = dot_nt(rp[d * 32 : d * 32 + 256, :], left) * (1.0 / ALL)
            block = block.astype(BF16)
            for e in range(8):
                for half in range(2):
                    at = pl.multiple_of(b * 64 + half * 32, 32)
                    om[pl.ds(at, 32), (d + e) * 128 : (d + e + 1) * 128] = block[
                        e * 32 : e * 32 + 32, half * 128 : half * 128 + 128
                    ]
        return carry

    lax.fori_loop(0, 8, outer, 0)

    def mid(b, carry):
        at = pl.multiple_of(b * 128, 128)
        update = dot(om[pl.ds(at, 128), :], wbd[...])
        for e in range(4):
            for a in range(4):
                i = b * 16 + e * 4 + a
                pm[i] = coup_ref[i] + update[e * 32 : e * 32 + 32, a * 128 : a * 128 + 128]
        return carry

    lax.fori_loop(0, 4, mid, 0)

    def entry(b, carry):
        pair = pm[pl.ds(b * 8, 8)].reshape(256, C_Z)
        pair = pair - jnp.mean(pair, axis=-1, keepdims=True)
        var = jnp.mean(pair * pair, axis=-1, keepdims=True)
        pair = (pair * lax.rsqrt(var + EPS)).astype(BF16)
        gp[pl.ds(b * 8, 8)] = jax.nn.sigmoid(dot(pair, wsw_ref[...])).reshape(8, RES, C_Z)
        entries = dot_nt(wit[...], pair)
        left = jax.nn.sigmoid(entries[128:256]) * entries[0:128]
        right = jax.nn.sigmoid(entries[384:512]) * entries[256:384]
        for half in range(2):
            lanes = slice(half * 128, half * 128 + 128)
            t = b * 2 + half
            cf[pl.ds(t, 128, stride=32), :] = left[:, lanes]
            cf[pl.ds(t + 16, 128, stride=32), :] = right[:, lanes]
        return carry

    lax.fori_loop(0, 8, entry, 0)
    cb[...] = cf[...].astype(BF16).reshape(DEVICES, 32, 128)

    corner = r * 4 + c // 4
    lanes_at = pl.multiple_of(lax.rem(c, 4) * 128, 128)

    def send_d(d, carry):
        peer = lax.rem(me + d, DEVICES)
        remote(
            cb.at[peer], xlr.at[corner, :, pl.ds(lanes_at, 128)], s_d, r_d,
            peer // COLS, lax.rem(peer, COLS),
        ).start()
        return carry

    lax.fori_loop(1, DEVICES, send_d, 0)
    pltpu.make_async_copy(cb.at[me], xlr.at[corner, :, pl.ds(lanes_at, 128)], r_d).start()

    arrived(gb, r_b)

    def refresh(n, carry):
        where = pl.ds(n, SEQ, stride=RES)
        change = dot(gb[n], wf_ref[...])
        for k in range(2):
            xs[k, where, :] = xs[k, where, :] + change[:, k * 128 : k * 128 + 128]
        return carry

    lax.fori_loop(0, RES, refresh, 0)
    store = [
        pltpu.make_async_copy(xs.at[k], out_m.at[:, pl.ds(k * 128, 128)], s_x.at[k])
        for k in range(2)
    ]
    store[0].start()
    store[1].start()

    arrived(xlr, r_d)

    def line_up(b, carry):
        moved = dot(xlr[pl.ds(b * 4, 4)].reshape(128, 512), perm[...]).astype(BF16)
        for e in range(4):
            for a in range(4):
                at = pl.multiple_of(b * 64 + a * 16, 16)
                lanes = slice(a * 128, a * 128 + 128)
                spot = slice(e * 128, e * 128 + 128)
                am[pl.ds(at, 16), spot] = moved[e * 32 : e * 32 + 16, lanes]
                bm[pl.ds(at, 16), spot] = moved[e * 32 + 16 : e * 32 + 32, lanes]
        return carry

    lax.fori_loop(0, 8, line_up, 0)
    pb[...] = dot_tn(am[...], bm[...]).astype(BF16)

    def deal(b, carry):
        for e in range(4):
            for a in range(4):
                at = pl.multiple_of(b * 64 + a * 16, 16)
                xe[e * 16 : e * 16 + 16, a * 128 : a * 128 + 128] = pb[
                    pl.ds(at, 16), e * 128 : e * 128 + 128
                ]
        es[pl.ds(b * 4, 4)] = dot(xe[...], perm[...]).astype(BF16).reshape(4, 16, 512)
        return carry

    lax.fori_loop(0, 8, deal, 0)

    def piece(peer):
        row, col = peer // COLS, lax.rem(peer, COLS)
        at = pl.multiple_of(lax.rem(col, 4) * 128, 128)
        return es.at[row * 4 + col // 4, :, pl.ds(at, 128)]

    def send_e(d, carry):
        peer = lax.rem(me + d, DEVICES)
        remote(
            piece(peer), er.at[me], s_e, r_e, peer // COLS, lax.rem(peer, COLS)
        ).start()
        return carry

    lax.fori_loop(1, DEVICES, send_e, 0)
    pltpu.make_async_copy(piece(me), er.at[me], r_e).start()
    arrived(er, r_e)

    ef[...] = er[...].astype(F32).reshape(DEVICES * 16, 128)

    def final(t, carry):
        prod = ef[pl.ds(t, DEVICES, stride=16), :]
        prod = prod - jnp.mean(prod, axis=0, keepdims=True)
        var = jnp.mean(prod * prod, axis=0, keepdims=True)
        prod = (prod * lax.rsqrt(var + EPS)).astype(BF16)
        update = dot_tn(prod, wtri_ref[...])
        for a in range(4):
            i = a * 16 + t
            out_p[i] = pm[i] + gp[i] * update[a * 32 : a * 32 + 32]
        return carry

    lax.fori_loop(0, 16, final, 0)

    store[0].wait()
    store[1].wait()
    for q in range(OWN):
        arrived(nt.at[q, pl.ds(0, 7)], s_a.at[q])
    arrived(sg.at[pl.ds(0, 7)], s_sig)
    arrived(gb.at[pl.ds(0, 28)], s_b)
    arrived(rb.at[pl.ds(0, 28)], s_r)

    @pl.when(rho == r)
    def _():
        arrived(lb.at[pl.ds(0, 60)], s_l)

    @pl.when(rho != r)
    def _():
        arrived(lb, s_l)

    arrived(cb.at[pl.ds(0, DEVICES - 1)], s_d)
    arrived(er.at[pl.ds(0, DEVICES - 1)], s_e)


def body(x, coup, wq, wx, wf, we, wo, wi, wsw, wtri):
    vmem = pl.BlockSpec(memory_space=pltpu.VMEM)
    hbm = pl.BlockSpec(memory_space=pl.ANY)
    dma = pltpu.SemaphoreType.DMA
    out_m, out_p = pl.pallas_call(
        kernel,
        out_shape=(
            jax.ShapeDtypeStruct((SEQ * RES, FEAT), F32),
            jax.ShapeDtypeStruct((SEQ, RES, C_Z), F32),
        ),
        in_specs=[hbm] + [vmem] * 9,
        out_specs=(hbm, vmem),
        scratch_shapes=[
            pltpu.VMEM((2, SEQ * RES, 128), F32),
            pltpu.VMEM((OWN, ROWS, SEQ, FEAT), BF16),
            pltpu.VMEM((OWN, ROWS, SEQ, FEAT), BF16),
            pltpu.VMEM((SEQ, 128), BF16),
            pltpu.VMEM((ROWS, SEQ, 128), BF16),
            pltpu.VMEM((ALL, FEAT), BF16),
            pltpu.VMEM((FEAT, ALL), BF16),
            pltpu.VMEM((ALL, FEAT), BF16),
            pltpu.VMEM((ALL, FEAT), F32),
            pltpu.VMEM((OWN, ROWS, SEQ, FEAT), BF16),
            pltpu.VMEM((RES, SEQ, FEAT), BF16),
            pltpu.VMEM((OWN, 64, ALL), BF16),
            pltpu.VMEM((RES, 32, ALL), BF16),
            pltpu.VMEM((SEQ, 32, ALL), BF16),
            pltpu.VMEM((64, FEAT), BF16),
            pltpu.VMEM((512, C_Z), BF16),
            pltpu.VMEM((1024, C_Z), F32),
            pltpu.VMEM((4096, 512), BF16),
            pltpu.VMEM((512, 512), BF16),
            pltpu.VMEM((4, 1024, 128), F32),
            pltpu.VMEM((1024, ALL), BF16),
            pltpu.VMEM((512, 4096), BF16),
            pltpu.VMEM((SEQ, RES, C_Z), F32),
            pltpu.VMEM((SEQ, RES, C_Z), F32),
            pltpu.VMEM((DEVICES * 32, 128), F32),
            pltpu.VMEM((DEVICES, 32, 128), BF16),
            pltpu.VMEM((32, 32, 512), BF16),
            pltpu.VMEM((512, 512), BF16),
            pltpu.VMEM((512, 512), BF16),
            pltpu.VMEM((512, 512), BF16),
            pltpu.VMEM((64, 512), BF16),
            pltpu.VMEM((32, 16, 512), BF16),
            pltpu.VMEM((DEVICES, 16, 128), BF16),
            pltpu.VMEM((DEVICES * 16, 128), F32),
            dma((2,)),
            dma((OWN,)), dma((OWN,)),
            dma(()), dma(()),
            dma(()), dma(()),
            dma(()), dma(()),
            dma(()), dma(()),
            dma(()), dma(()),
            dma(()), dma(()),
        ],
        compiler_params=pltpu.CompilerParams(
            collective_id=0, has_side_effects=True, vmem_limit_bytes=56 * 2**20
        ),
    )(x.reshape(SEQ * RES, FEAT), coup, wq, wx, wf, we, wo, wi, wsw, wtri)
    return out_m.reshape(SEQ, RES, FEAT), out_p


def solution(mesh):
    spread = P("row", "col", None)
    return jax.shard_map(
        body, mesh=mesh, in_specs=(spread, spread) + (P(),) * 8,
        out_specs=(spread, spread), check_vma=False,
    )
```

time: 801 us -> 270 us (0.34)
  waiting for transfers between devices: 570 us -> 0 us
  Pallas kernels: 0 us -> 262 us
  local copies, waits for them, and re-layouts: 74.8 us -> 5.71 us
  matrix products: 64.6 us -> 0 us
  other arithmetic: 34.1 us -> 0 us
  blocking collectives: 27.1 us -> 0 us
  between operations: 14.7 us -> 0.65 us
    psum x2 -> x0, waiting for transfers between devices: 313 us -> none  [broadcast(): return lax.psum(block, axis)]
    pallas_call x0 -> x1, Pallas kernels: none -> 262 us  [body(): pl.pallas_call(kernel, out_shape=(jax.ShapeDtypeStruct((SEQ * RES, FEAT),...]
    all_gather x4 -> x0, waiting for transfers between devices: 242 us -> none  [the longest x1 89.9 us: route_pair(): lax.all_gather(left_piece, 'row', axis=0, tiled=True)]
    dot_general x20 -> x0, matrix products: 54.5 us -> none  [the longest x4 13.2 us: attend_column(): jnp.einsum('hst,thd->shd', weights, value_rows, preferred_element_type=jn...]
    convert_element_type x5 -> x0, local copies, waits for them, and re-layouts: 44.2 us -> none  [the longest x2 42.1 us: body(): outer_mean = (outer_product_sum / total_seqs).astype(jnp.bfloat16)]
    all_to_all x1 -> x0, blocking collectives: 27.1 us -> none  [body(): lax.all_to_all(jnp.transpose(attended, (1, 0, 2)), 'row', split_axis=0, c...]
    all_to_all x1 -> x0, waiting for transfers between devices: 15.1 us -> none  [body(): lax.all_to_all(standardised, 'row', split_axis=1, concat_axis=0, tiled=True)]
    all_gather x2 -> x0, local copies, waits for them, and re-layouts: 13 us -> none  [the longest x1 6.5 us: route_pair(): lax.all_gather(left_piece, 'row', axis=0, tiled=True)]
  transfers between devices with their start and end apart: 7 -> 0, of which waited for: 7 -> 0; matrix products, arithmetic and copies ran while one was open for 3% -> 0% of each run, Pallas kernels for 0% -> 0%
where the time goes in v1:
time: 270 us; the launch traced here: 269 us
  Pallas kernels  262 us (97%)
  local copies, waits for them, and re-layouts  5.71 us (2%)
    pallas_call x1, Pallas kernels, body(): pl.pallas_call(kernel, out_shape=(jax.ShapeDtypeStruct((SEQ * RES, FEAT),...  262 us
    unnamed x5, local copies, waits for them, and re-layouts  5.71 us

profile of v1, /device:TPU:1, one launch (start us, length us, event | category | flops | bytes accessed | tf_op | source)
XLA Modules:
  0.0 268.7 jit_solution(13285743994944041397)
XLA Ops:
  0.6 1.5 copy.12.we_ref
  2.1 262.3 %shard_map.113 = (f32[2048,256]{1,0:T(8,128)}, f32[64,32,128]{2,1,0:T(8,128)}) custom-call(f32[2048,256]{1,0:T(8,128)} %bitcast.2, f32[64,32,128]{2,1,0:T(8,128)} %coup_ref.1, bf16[256,256]{1,0:T(8,128)(2,1)} %wq_ref.1, bf16[256,768]{1,0:T(8,128)(2,1)} %wx_ref.1, bf16[256,256]{1,0:T(8,128)(2,1)} %wf_ref.1, bf16[256,64]{1,0:T(8,128)(2,1)} %copy.12.we_ref, ...), custom_call_target="tpu_custom_call" | custom-call | tf_op jit(solution)/shard_map/pallas_call | solution.py:393
  264.4 0.0 copy-start
  264.4 3.2 %copy.15 = f32[64,32,256]{2,1,0:T(8,128)} copy(f32[64,32,256]{2,1,0:T(8,128)} %bitcast.3) | data formatting | bytes 4194304
  267.7 0.0 copy-done
  267.7 1.0 copy.16
Async XLA Ops:
  264.4 3.3 %copy-start = (f32[64,32,128]{2,1,0:T(8,128)S(1)}, f32[64,32,128]{2,1,0:T(8,128)}, u32[]{:S(2)}) copy-start(f32[64,32,128]{2,1,0:T(8,128)} %get-tuple-element.9) | copy-start | bytes 3145732

commit v2 on v1

--- a/solution.py
+++ b/solution.py
@@ -43,8 +43,8 @@
     x_ref, coup_ref, wq_ref, wx_ref, wf_ref, we_ref, wo_ref, wi_ref, wsw_ref, wtri_ref,
     out_m, out_p,
     xs, nt, g, sig, sg, qs, kt, vs, ga, gt, gb, lrs, rb, lb,
-    wet, wit, wof, wbd, perm, rf, rp, om, pm, gp, cf, cb, xlr, am, bm, pb, xe, es, er, ef,
-    s_x, s_a, r_a, s_sig, r_sig, s_b, r_b, s_l, r_l, s_r, r_r, s_d, r_d, s_e, r_e,
+    wit, wof, wbd, perm, rf, rp, om, pm, gp, cf, cb, xlr, am, bm, pb, xe, es, er, ef,
+    s_x, s_a, r_a, s_sig, r_sig, s_b, r_b, s_h, r_h, s_l, r_l, s_r, r_r, s_d, r_d, s_e, r_e,
 ):
     r = lax.axis_index("row")
     c = lax.axis_index("col")
@@ -118,7 +118,6 @@
     lax.fori_loop(1, ROWS, send_sig, 0)
     pltpu.make_async_copy(sig, sg.at[r], r_sig).start()
 
-    wet[...] = we_ref[...].astype(F32).T.astype(BF16)
     wit[...] = wi_ref[...].astype(F32).T.astype(BF16)
     wof[...] = wo_ref[...].astype(F32)
     wbd[...] = jnp.zeros(wbd.shape, BF16)
@@ -135,6 +134,18 @@
     target = ((source >> 5) & 3) * 128 + (source >> 7) * 32 + (source & 31)
     column = lax.broadcasted_iota(jnp.int32, (512, 512), 1)
     perm[...] = jnp.where(column == target, 1.0, 0.0).astype(BF16)
+
+    def relay(q):
+        arrived(lb.at[pl.ds(0, 2)], r_h.at[q])
+
+        def pass_on(j, carry):
+            col = c // 8 * 8 + lax.rem(c + j, 8)
+            for side in range(2):
+                spot = q * 16 + side * 8 + lax.rem(c, 8)
+                remote(lb.at[spot], lb.at[spot], s_l, r_l.at[q], r, col).start()
+            return carry
+
+        lax.fori_loop(1, 8, pass_on, 0)
 
     def attend(q, carry):
         arrived(g.at[q], r_a.at[q])
@@ -144,6 +155,12 @@
         vs[...] = dot(column, wx_ref[:, 256:512]).astype(BF16)
         ga[...] = jax.nn.sigmoid(dot(column, wx_ref[:, 512:768]))
         for tile in range(2):
+            if tile == 1:
+
+                @pl.when(q > 0)
+                def _():
+                    relay(q - 1)
+
             cols = slice(tile * 128, tile * 128 + 128)
             for part in range(2):
                 rows = slice(part * 256, part * 256 + 256)
@@ -183,7 +200,7 @@
             fresh = fresh - jnp.mean(fresh, axis=-1, keepdims=True)
             var = jnp.mean(fresh * fresh, axis=-1, keepdims=True)
             fresh = (fresh * (sd * lax.rsqrt(sd * sd * var + EPS))).astype(BF16)
-            lrs[q, :, rows] = dot_nt(wet[...], fresh).astype(BF16)
+            lrs[q, :, rows] = dot_nt(we_ref[...], fresh).astype(BF16)
 
         def send_r(j, carry):
             row = lax.rem(r + j, ROWS)
@@ -192,22 +209,19 @@
 
         lax.fori_loop(1, ROWS, send_r, 0)
         pltpu.make_async_copy(lrs.at[q, pl.ds(32, 32)], rb.at[r * OWN + q], r_r).start()
-        spot = lax.rem(c, 2) * RES + r * OWN + q
-
-        def send_l(j, carry):
-            col = lax.rem(c + j, COLS)
-            remote(lrs.at[q, pl.ds(0, 32)], lb.at[spot], s_l, r_l, rho, col).start()
-            return carry
-
-        lax.fori_loop(1, COLS, send_l, 0)
-
-        @pl.when(rho == r)
-        def _():
-            pltpu.make_async_copy(lrs.at[q, pl.ds(0, 32)], lb.at[spot], r_l).start()
-
-        @pl.when(rho != r)
-        def _():
-            remote(lrs.at[q, pl.ds(0, 32)], lb.at[spot], s_l, r_l, rho, c).start()
+        spot = q * 16 + lax.rem(c, 2) * ROWS + r
+        for half in range(2):
+            here = jnp.logical_and(rho == r, c == half * 8 + r)
+
+            @pl.when(here)
+            def _():
+                pltpu.make_async_copy(lrs.at[q, pl.ds(0, 32)], lb.at[spot], r_h.at[q]).start()
+
+            @pl.when(jnp.logical_not(here))
+            def _():
+                remote(
+                    lrs.at[q, pl.ds(0, 32)], lb.at[spot], s_h, r_h.at[q], rho, half * 8 + r
+                ).start()
 
         lax.fori_loop(1, ROWS, send_b, 0)
         pltpu.make_async_copy(gt.at[q, r], gb.at[r * OWN + q], r_b).start()
@@ -229,7 +243,7 @@
 
     lax.fori_loop(0, 32, by_channel, 0)
 
-    arrived(lb, r_l)
+    relay(OWN - 1)
 
     def outer(b, carry):
         left = lb[pl.ds(b * 8, 8)].reshape(256, ALL)
@@ -244,18 +258,14 @@
                     ]
         return carry
 
-    lax.fori_loop(0, 8, outer, 0)
-
     def mid(b, carry):
         at = pl.multiple_of(b * 128, 128)
         update = dot(om[pl.ds(at, 128), :], wbd[...])
         for e in range(4):
             for a in range(4):
-                i = b * 16 + e * 4 + a
-                pm[i] = coup_ref[i] + update[e * 32 : e * 32 + 32, a * 128 : a * 128 + 128]
-        return carry
-
-    lax.fori_loop(0, 4, mid, 0)
+                i = e // 2 * 32 + (e % 2 * 4 + a) * 4 + b
+                pm[b * 16 + e * 4 + a] = coup_ref[i] + update[e * 32 : e * 32 + 32, a * 128 : a * 128 + 128]
+        return carry
 
     def entry(b, carry):
         pair = pm[pl.ds(b * 8, 8)].reshape(256, C_Z)
@@ -273,7 +283,14 @@
             cf[pl.ds(t + 16, 128, stride=32), :] = right[:, lanes]
         return carry
 
-    lax.fori_loop(0, 8, entry, 0)
+    def pairs(q, carry):
+        arrived(lb.at[pl.ds(0, 14)], r_l.at[q])
+        lax.fori_loop(q * 2, q * 2 + 2, outer, 0)
+        mid(q, 0)
+        lax.fori_loop(q * 2, q * 2 + 2, entry, 0)
+        return carry
+
+    lax.fori_loop(0, OWN, pairs, 0)
     cb[...] = cf[...].astype(BF16).reshape(DEVICES, 32, 128)
 
     corner = r * 4 + c // 4
@@ -360,8 +377,8 @@
         prod = (prod * lax.rsqrt(var + EPS)).astype(BF16)
         update = dot_tn(prod, wtri_ref[...])
         for a in range(4):
-            i = a * 16 + t
-            out_p[i] = pm[i] + gp[i] * update[a * 32 : a * 32 + 32]
+            p = lax.rem(t, 4) * 16 + a * 4 + t // 4
+            out_p[a * 16 + t] = pm[p] + gp[p] * update[a * 32 : a * 32 + 32]
         return carry
 
     lax.fori_loop(0, 16, final, 0)
@@ -374,14 +391,17 @@
     arrived(gb.at[pl.ds(0, 28)], s_b)
     arrived(rb.at[pl.ds(0, 28)], s_r)
 
-    @pl.when(rho == r)
+    relays_itself = jnp.logical_and(rho == r, lax.rem(c, 8) == r)
+
+    @pl.when(relays_itself)
     def _():
-        arrived(lb.at[pl.ds(0, 60)], s_l)
-
-    @pl.when(rho != r)
+        arrived(lb.at[pl.ds(0, 4)], s_h)
+
+    @pl.when(jnp.logical_not(relays_itself))
     def _():
-        arrived(lb, s_l)
-
+        arrived(lb.at[pl.ds(0, 8)], s_h)
+
+    arrived(lb.at[pl.ds(0, 56)], s_l)
     arrived(cb.at[pl.ds(0, DEVICES - 1)], s_d)
     arrived(er.at[pl.ds(0, DEVICES - 1)], s_e)
 
@@ -413,7 +433,6 @@
             pltpu.VMEM((OWN, 64, ALL), BF16),
             pltpu.VMEM((RES, 32, ALL), BF16),
             pltpu.VMEM((SEQ, 32, ALL), BF16),
-            pltpu.VMEM((64, FEAT), BF16),
             pltpu.VMEM((512, C_Z), BF16),
             pltpu.VMEM((1024, C_Z), F32),
             pltpu.VMEM((4096, 512), BF16),
@@ -437,7 +456,8 @@
             dma((OWN,)), dma((OWN,)),
             dma(()), dma(()),
             dma(()), dma(()),
-            dma(()), dma(()),
+            dma(()), dma((OWN,)),
+            dma(()), dma((OWN,)),
             dma(()), dma(()),
             dma(()), dma(()),
             dma(()), dma(()),
@@ -445,7 +465,7 @@
         compiler_params=pltpu.CompilerParams(
             collective_id=0, has_side_effects=True, vmem_limit_bytes=56 * 2**20
         ),
-    )(x.reshape(SEQ * RES, FEAT), coup, wq, wx, wf, we, wo, wi, wsw, wtri)
+    )(x.reshape(SEQ * RES, FEAT), coup, wq, wx, wf, we.T, wo, wi, wsw, wtri)
     return out_m.reshape(SEQ, RES, FEAT), out_p
 
 

time: 270 us -> 130 us (0.48)
  Pallas kernels: 262 us -> 125 us
    pallas_call x1, Pallas kernels: 262 us -> 125 us  [body(): pl.pallas_call(kernel, out_shape=(jax.ShapeDtypeStruct((SEQ * RES, FEAT),...]
    unnamed x5 -> x4, local copies, waits for them, and re-layouts: 5.71 us -> 4.22 us
where the time goes in v2:
time: 130 us
  Pallas kernels  125 us (96%)
  local copies, waits for them, and re-layouts  4.22 us (3%)
    pallas_call x1, Pallas kernels, body(): pl.pallas_call(kernel, out_shape=(jax.ShapeDtypeStruct((SEQ * RES, FEAT),...  125 us
    unnamed x4, local copies, waits for them, and re-layouts  4.22 us

profile of v2, /device:TPU:1, one launch (start us, length us, event | category | flops | bytes accessed | tf_op | source)
XLA Modules:
  0.0 130.1 jit_solution(10018126351360427387)
XLA Ops:
  0.6 125.2 %shard_map.113 = (f32[2048,256]{1,0:T(8,128)}, f32[64,32,128]{2,1,0:T(8,128)}) custom-call(f32[2048,256]{1,0:T(8,128)} %bitcast.3, f32[64,32,128]{2,1,0:T(8,128)} %coup_ref.1, bf16[256,256]{1,0:T(8,128)(2,1)} %wq_ref.1, bf16[256,768]{1,0:T(8,128)(2,1)} %wx_ref.1, bf16[256,256]{1,0:T(8,128)(2,1)} %wf_ref.1, bf16[64,256]{1,0:T(8,128)(2,1)} %bitcast.5, ...), custom_call_target="tpu_custom_call" | custom-call | tf_op jit(solution)/shard_map/pallas_call | solution.py:413
  125.9 0.0 copy-start
  125.9 3.2 %copy.14 = f32[64,32,256]{2,1,0:T(8,128)} copy(f32[64,32,256]{2,1,0:T(8,128)} %bitcast.4) | data formatting | bytes 4194304
  129.1 0.0 copy-done
  129.1 1.0 copy.15
Async XLA Ops:
  125.9 3.3 %copy-start = (f32[64,32,128]{2,1,0:T(8,128)S(1)}, f32[64,32,128]{2,1,0:T(8,128)}, u32[]{:S(2)}) copy-start(f32[64,32,128]{2,1,0:T(8,128)} %get-tuple-element.9) | copy-start | bytes 3145732

commit v3 on v2

--- a/solution.py
+++ b/solution.py
@@ -10,6 +10,7 @@
 F32, BF16 = jnp.float32, jnp.bfloat16
 MESH = pl.DeviceIdType.MESH
 EPS = 1e-05
+LOG2E = 1.4426950408889634
 ROWS, COLS = 8, 16
 DEVICES = ROWS * COLS
 SEQ, RES = 64, 32
@@ -43,8 +44,8 @@
     x_ref, coup_ref, wq_ref, wx_ref, wf_ref, we_ref, wo_ref, wi_ref, wsw_ref, wtri_ref,
     out_m, out_p,
     xs, nt, g, sig, sg, qs, kt, vs, ga, gt, gb, lrs, rb, lb,
-    wit, wof, wbd, perm, rf, rp, om, pm, gp, cf, cb, xlr, am, bm, pb, xe, es, er, ef,
-    s_x, s_a, r_a, s_sig, r_sig, s_b, r_b, s_h, r_h, s_l, r_l, s_r, r_r, s_d, r_d, s_e, r_e,
+    wit, wof, wbd, perm, rf, rp, om, pm, gp, cf, cb, xlr, am, bm, pa, pb, xe, es, er, ef,
+    s_x, s_a, r_a, s_sig, r_sig, s_b, r_b, s_h, r_h, s_l, r_l, s_c, r_c, s_r, r_r, s_d, r_d, s_e, r_e,
 ):
     r = lax.axis_index("row")
     c = lax.axis_index("col")
@@ -95,28 +96,27 @@
 
     load[0].wait()
     load[1].wait()
-    stats = jnp.zeros((SEQ, 128), F32)
-    for q in range(OWN):
-        stats = lax.fori_loop(0, ROWS, lambda row, s, q=q: norm_one(q, row, s), stats)
-        if q == 0:
-            pl.semaphore_wait(barrier, DEVICES - 1)
-
-        def send_a(j, carry, q=q):
+    def send_normed(q):
+        def send_a(j, carry):
             row = lax.rem(r + j, ROWS)
             remote(nt.at[q, row], g.at[q, r], s_a.at[q], r_a.at[q], row, c).start()
             return carry
 
         lax.fori_loop(1, ROWS, send_a, 0)
         pltpu.make_async_copy(nt.at[q, r], g.at[q, r], r_a.at[q]).start()
-    sig[...] = stats.astype(BF16)
 
     def send_sig(j, carry):
         row = lax.rem(r + j, ROWS)
         remote(sig, sg.at[r], s_sig, r_sig, row, c).start()
         return carry
 
-    lax.fori_loop(1, ROWS, send_sig, 0)
-    pltpu.make_async_copy(sig, sg.at[r], r_sig).start()
+    stats = jnp.zeros((SEQ, 128), F32)
+    for q in range(OWN):
+        stats = lax.fori_loop(0, ROWS, lambda row, s, q=q: norm_one(q, row, s), stats, unroll=4)
+        if q == 0:
+            pl.semaphore_wait(barrier, DEVICES - 1)
+            send_normed(0)
+    sig[...] = stats.astype(BF16)
 
     wit[...] = wi_ref[...].astype(F32).T.astype(BF16)
     wof[...] = wo_ref[...].astype(F32)
@@ -135,54 +135,71 @@
     column = lax.broadcasted_iota(jnp.int32, (512, 512), 1)
     perm[...] = jnp.where(column == target, 1.0, 0.0).astype(BF16)
 
+    core = lax.rem(c, 2)
+
     def relay(q):
         arrived(lb.at[pl.ds(0, 2)], r_h.at[q])
+        mine = lb.at[pl.ds(q * 16 + core * 8 + lax.rem(c, 8) // 2 * 2, 2)]
 
         def pass_on(j, carry):
-            col = c // 8 * 8 + lax.rem(c + j, 8)
-            for side in range(2):
-                spot = q * 16 + side * 8 + lax.rem(c, 8)
-                remote(lb.at[spot], lb.at[spot], s_l, r_l.at[q], r, col).start()
+            col = c // 8 * 8 + lax.rem(c + 2 * j, 8)
+            remote(mine, mine, s_l, r_l.at[q], r, col).start()
             return carry
 
-        lax.fori_loop(1, 8, pass_on, 0)
+        lax.fori_loop(1, 4, pass_on, 0)
+
+    def send_gated(q):
+        def send_b(j, carry):
+            row = lax.rem(r + j, ROWS)
+            remote(gt.at[q, row], gb.at[r * OWN + q], s_b, r_b, row, c).start()
+            return carry
+
+        lax.fori_loop(1, ROWS, send_b, 0)
+        pltpu.make_async_copy(gt.at[q, r], gb.at[r * OWN + q], r_b).start()
+
+    def share(q):
+        arrived(lb.at[pl.ds(0, 6)], r_l.at[q])
+        mine = lb.at[pl.ds(q * 16 + core * 8, 8)]
+        remote(mine, mine, s_c, r_c.at[q], r, c + 1 - 2 * core).start()
 
     def attend(q, carry):
         arrived(g.at[q], r_a.at[q])
+
+        @pl.when(q < OWN - 1)
+        def _():
+            send_normed(q + 1)
+
+        @pl.when(q == 0)
+        def _():
+            lax.fori_loop(1, ROWS, send_sig, 0)
+            pltpu.make_async_copy(sig, sg.at[r], r_sig).start()
+
         column = g[q].reshape(ALL, FEAT)
-        qs[...] = (dot(column, wq_ref[...]) * 32 ** (-0.5)).astype(BF16)
+        qs[...] = (dot(column, wq_ref[...]) * (32 ** (-0.5) * LOG2E)).astype(BF16)
         kt[...] = dot(column, wx_ref[:, 0:256]).T.astype(BF16)
         vs[...] = dot(column, wx_ref[:, 256:512]).astype(BF16)
         ga[...] = jax.nn.sigmoid(dot(column, wx_ref[:, 512:768]))
         for tile in range(2):
-            if tile == 1:
-
-                @pl.when(q > 0)
-                def _():
-                    relay(q - 1)
-
             cols = slice(tile * 128, tile * 128 + 128)
+            masks = [head_mask(128, h) for h in range(4)]
+            values = jnp.concatenate(
+                [
+                    jnp.concatenate(
+                        [vs[:, cols] * mask, jnp.broadcast_to(mask, (ALL, 128))], axis=1
+                    )
+                    for mask in masks
+                ]
+            )
             for part in range(2):
                 rows = slice(part * 256, part * 256 + 256)
-                top = jnp.zeros((256, 128), F32)
-                low = jnp.ones((256, 128), F32)
+                weights = []
                 for h in range(4):
-                    mask = head_mask(128, h)
-                    values = vs[:, cols] * mask + (1 - mask)
                     scores = dot(qs[rows, :] * head_mask(256, tile * 4 + h), kt[...])
                     best = jnp.max(scores, axis=-1, keepdims=True)
-                    weights = jnp.exp(scores - best).astype(BF16)
-                    found = dot(weights, values)
-                    here = (lane(128) >> 5) == h
-                    top = jnp.where(here, found, top)
-                    low = jnp.where(here, pltpu.roll(found, 32, 1), low)
-                gated = (top / low * ga[rows, cols]).astype(BF16)
+                    weights.append(jnp.exp2(scores - best).astype(BF16))
+                found = dot(jnp.concatenate(weights, axis=1), values)
+                gated = (found[:, :128] / found[:, 128:] * ga[rows, cols]).astype(BF16)
                 gt[q, part * 4 : part * 4 + 4, :, cols] = gated.reshape(4, SEQ, 128)
-
-        def send_b(j, carry):
-            row = lax.rem(r + j, ROWS)
-            remote(gt.at[q, row], gb.at[r * OWN + q], s_b, r_b, row, c).start()
-            return carry
 
         @pl.when(q == 0)
         def _():
@@ -202,14 +219,7 @@
             fresh = (fresh * (sd * lax.rsqrt(sd * sd * var + EPS))).astype(BF16)
             lrs[q, :, rows] = dot_nt(we_ref[...], fresh).astype(BF16)
 
-        def send_r(j, carry):
-            row = lax.rem(r + j, ROWS)
-            remote(lrs.at[q, pl.ds(32, 32)], rb.at[r * OWN + q], s_r, r_r, row, c).start()
-            return carry
-
-        lax.fori_loop(1, ROWS, send_r, 0)
-        pltpu.make_async_copy(lrs.at[q, pl.ds(32, 32)], rb.at[r * OWN + q], r_r).start()
-        spot = q * 16 + lax.rem(c, 2) * ROWS + r
+        spot = q * 16 + lax.rem(r, 2) * 8 + r // 2 * 2 + lax.rem(c, 2)
         for half in range(2):
             here = jnp.logical_and(rho == r, c == half * 8 + r)
 
@@ -223,27 +233,44 @@
                     lrs.at[q, pl.ds(0, 32)], lb.at[spot], s_h, r_h.at[q], rho, half * 8 + r
                 ).start()
 
-        lax.fori_loop(1, ROWS, send_b, 0)
-        pltpu.make_async_copy(gt.at[q, r], gb.at[r * OWN + q], r_b).start()
+        def send_r(j, carry):
+            row = lax.rem(r + j, ROWS)
+            remote(
+                lrs.at[q, pl.ds(32, 32)], rb.at[r * OWN + q], s_r, r_r.at[q], row, c
+            ).start()
+            return carry
+
+        lax.fori_loop(1, ROWS, send_r, 0)
+        pltpu.make_async_copy(lrs.at[q, pl.ds(32, 32)], rb.at[r * OWN + q], r_r.at[q]).start()
+        @pl.when(q > 0)
+        def _():
+            relay(q - 1)
+
+        @pl.when(q > 1)
+        def _():
+            share(q - 2)
+
         return carry
 
     lax.fori_loop(0, OWN, attend, 0)
 
-    arrived(rb, r_r)
+    def by_channel(row, q):
+        n = row * OWN + q
+        for k in range(4):
+            rf[k, pl.ds(n, 32, stride=32), :] = rb[n, :, k * 128 : k * 128 + 128].astype(F32)
+        return q
+
+    for q in range(OWN):
+        if q == OWN - 1:
+            relay(OWN - 1)
+            share(OWN - 2)
+        arrived(rb.at[pl.ds(0, ROWS)], r_r.at[q])
+        lax.fori_loop(0, ROWS, by_channel, q, unroll=2)
     for k in range(4):
-        rf[k] = rb[:, :, k * 128 : k * 128 + 128].astype(F32).reshape(1024, 128)
-
-    def by_channel(d, carry):
-        at = pl.multiple_of(d * 32, 32)
-        for k in range(4):
-            rp[pl.ds(at, 32), k * 128 : k * 128 + 128] = rf[
-                k, pl.ds(d, 32, stride=32), :
-            ].astype(BF16)
-        return carry
-
-    lax.fori_loop(0, 32, by_channel, 0)
-
-    relay(OWN - 1)
+        rp[:, k * 128 : k * 128 + 128] = rf[k].astype(BF16)
+
+    for q in range(OWN):
+        send_gated(q)
 
     def outer(b, carry):
         left = lb[pl.ds(b * 8, 8)].reshape(256, ALL)
@@ -258,14 +285,15 @@
                     ]
         return carry
 
-    def mid(b, carry):
-        at = pl.multiple_of(b * 128, 128)
-        update = dot(om[pl.ds(at, 128), :], wbd[...])
-        for e in range(4):
+    def mid(b):
+        update = dot(om[b * 256 : b * 256 + 256, :], wbd[...])
+        for f in range(8):
             for a in range(4):
-                i = e // 2 * 32 + (e % 2 * 4 + a) * 4 + b
-                pm[b * 16 + e * 4 + a] = coup_ref[i] + update[e * 32 : e * 32 + 32, a * 128 : a * 128 + 128]
-        return carry
+                e, q = f % 4, b * 2 + f // 4
+                i = a % 2 * 32 + (e % 2 * 4 + a // 2 * 2 + e // 2) * 4 + q
+                pm[q * 16 + e * 4 + a] = (
+                    coup_ref[i] + update[f * 32 : f * 32 + 32, a * 128 : a * 128 + 128]
+                )
 
     def entry(b, carry):
         pair = pm[pl.ds(b * 8, 8)].reshape(256, C_Z)
@@ -278,45 +306,57 @@
         right = jax.nn.sigmoid(entries[384:512]) * entries[256:384]
         for half in range(2):
             lanes = slice(half * 128, half * 128 + 128)
-            t = b * 2 + half
-            cf[pl.ds(t, 128, stride=32), :] = left[:, lanes]
-            cf[pl.ds(t + 16, 128, stride=32), :] = right[:, lanes]
-        return carry
-
-    def pairs(q, carry):
-        arrived(lb.at[pl.ds(0, 14)], r_l.at[q])
-        lax.fori_loop(q * 2, q * 2 + 2, outer, 0)
-        mid(q, 0)
-        lax.fori_loop(q * 2, q * 2 + 2, entry, 0)
-        return carry
-
-    lax.fori_loop(0, OWN, pairs, 0)
-    cb[...] = cf[...].astype(BF16).reshape(DEVICES, 32, 128)
+            t = lax.rem(b, 4) * 2 + half
+            cf[b // 4, pl.ds(t, 128, stride=16), :] = left[:, lanes]
+            cf[b // 4, pl.ds(t + 8, 128, stride=16), :] = right[:, lanes]
+        return carry
 
     corner = r * 4 + c // 4
     lanes_at = pl.multiple_of(lax.rem(c, 4) * 128, 128)
 
-    def send_d(d, carry):
-        peer = lax.rem(me + d, DEVICES)
-        remote(
-            cb.at[peer], xlr.at[corner, :, pl.ds(lanes_at, 128)], s_d, r_d,
-            peer // COLS, lax.rem(peer, COLS),
+    def pairs(half):
+        for q in (half * 2, half * 2 + 1):
+            arrived(lb.at[pl.ds(0, 8)], r_c.at[q])
+            lax.fori_loop(q * 2, q * 2 + 2, outer, 0)
+            if q == OWN - 2:
+                share(OWN - 1)
+        mid(half)
+        lax.fori_loop(half * 4, half * 4 + 4, entry, 0)
+
+    def deal_out(half):
+        cb[half] = cf[half].astype(BF16).reshape(DEVICES, 16, 128)
+
+        def send_d(d, carry):
+            peer = lax.rem(me + d, DEVICES)
+            remote(
+                cb.at[half, peer], xlr.at[half, corner, :, pl.ds(lanes_at, 128)],
+                s_d.at[half], r_d.at[half], peer // COLS, lax.rem(peer, COLS),
+            ).start()
+            return carry
+
+        lax.fori_loop(1, DEVICES, send_d, 0)
+        pltpu.make_async_copy(
+            cb.at[half, me], xlr.at[half, corner, :, pl.ds(lanes_at, 128)], r_d.at[half]
         ).start()
-        return carry
-
-    lax.fori_loop(1, DEVICES, send_d, 0)
-    pltpu.make_async_copy(cb.at[me], xlr.at[corner, :, pl.ds(lanes_at, 128)], r_d).start()
+
+    pairs(0)
+    deal_out(0)
+    pairs(1)
+    deal_out(1)
 
     arrived(gb, r_b)
 
-    def refresh(n, carry):
-        where = pl.ds(n, SEQ, stride=RES)
-        change = dot(gb[n], wf_ref[...])
-        for k in range(2):
-            xs[k, where, :] = xs[k, where, :] + change[:, k * 128 : k * 128 + 128]
-        return carry
-
-    lax.fori_loop(0, RES, refresh, 0)
+    def refresh(b, carry):
+        change = dot(gb[pl.ds(b * 4, 4)].reshape(256, FEAT), wf_ref[...])
+        for e in range(4):
+            where = pl.ds(b * 4 + e, SEQ, stride=RES)
+            for k in range(2):
+                xs[k, where, :] = (
+                    xs[k, where, :] + change[e * 64 : e * 64 + 64, k * 128 : k * 128 + 128]
+                )
+        return carry
+
+    lax.fori_loop(0, RES // 4, refresh, 0)
     store = [
         pltpu.make_async_copy(xs.at[k], out_m.at[:, pl.ds(k * 128, 128)], s_x.at[k])
         for k in range(2)
@@ -324,48 +364,57 @@
     store[0].start()
     store[1].start()
 
-    arrived(xlr, r_d)
-
-    def line_up(b, carry):
-        moved = dot(xlr[pl.ds(b * 4, 4)].reshape(128, 512), perm[...]).astype(BF16)
+    def line_up(b, half):
+        moved = dot(xlr[half, pl.ds(b * 8, 8)].reshape(128, 512), perm[...])
         for e in range(4):
             for a in range(4):
-                at = pl.multiple_of(b * 64 + a * 16, 16)
+                at = pl.multiple_of(half * 256 + b * 64 + a * 16, 16)
                 lanes = slice(a * 128, a * 128 + 128)
                 spot = slice(e * 128, e * 128 + 128)
-                am[pl.ds(at, 16), spot] = moved[e * 32 : e * 32 + 16, lanes]
-                bm[pl.ds(at, 16), spot] = moved[e * 32 + 16 : e * 32 + 32, lanes]
-        return carry
-
-    lax.fori_loop(0, 8, line_up, 0)
-    pb[...] = dot_tn(am[...], bm[...]).astype(BF16)
+                one, two = moved[e * 16 : e * 16 + 16, lanes], moved[e * 16 + 64 : e * 16 + 80, lanes]
+                am[pl.ds(at, 16), spot] = jnp.concatenate([one[:8], two[:8]]).astype(BF16)
+                bm[pl.ds(at, 16), spot] = jnp.concatenate([one[8:], two[8:]]).astype(BF16)
+        return half
+
+    arrived(xlr.at[0], r_d.at[0])
+    lax.fori_loop(0, 4, line_up, 0)
+    pa[...] = dot_tn(am[0:256, :], bm[0:256, :])
+    arrived(xlr.at[1], r_d.at[1])
+    lax.fori_loop(0, 4, line_up, 1)
+    pb[...] = (pa[...] + dot_tn(am[256:512, :], bm[256:512, :])).astype(BF16)
 
     def deal(b, carry):
+        row = lax.rem(r + b, ROWS)
         for e in range(4):
             for a in range(4):
-                at = pl.multiple_of(b * 64 + a * 16, 16)
+                at = pl.multiple_of(row * 64 + a * 16, 16)
                 xe[e * 16 : e * 16 + 16, a * 128 : a * 128 + 128] = pb[
                     pl.ds(at, 16), e * 128 : e * 128 + 128
                 ]
-        es[pl.ds(b * 4, 4)] = dot(xe[...], perm[...]).astype(BF16).reshape(4, 16, 512)
-        return carry
-
-    lax.fori_loop(0, 8, deal, 0)
-
-    def piece(peer):
-        row, col = peer // COLS, lax.rem(peer, COLS)
-        at = pl.multiple_of(lax.rem(col, 4) * 128, 128)
-        return es.at[row * 4 + col // 4, :, pl.ds(at, 128)]
-
-    def send_e(d, carry):
-        peer = lax.rem(me + d, DEVICES)
-        remote(
-            piece(peer), er.at[me], s_e, r_e, peer // COLS, lax.rem(peer, COLS)
-        ).start()
-        return carry
-
-    lax.fori_loop(1, DEVICES, send_e, 0)
-    pltpu.make_async_copy(piece(me), er.at[me], r_e).start()
+        es[pl.ds(row * 4, 4)] = dot(xe[...], perm[...]).astype(BF16).reshape(4, 16, 512)
+
+        def piece(col):
+            at = pl.multiple_of(lax.rem(col, 4) * 128, 128)
+            return es.at[row * 4 + col // 4, :, pl.ds(at, 128)]
+
+        def send_e(j, inner):
+            col = lax.rem(c + j, COLS)
+            remote(piece(col), er.at[me], s_e, r_e, row, col).start()
+            return inner
+
+        lax.fori_loop(1, COLS, send_e, 0)
+
+        @pl.when(b == 0)
+        def _():
+            pltpu.make_async_copy(piece(c), er.at[me], r_e).start()
+
+        @pl.when(b > 0)
+        def _():
+            remote(piece(c), er.at[me], s_e, r_e, row, c).start()
+
+        return carry
+
+    lax.fori_loop(0, ROWS, deal, 0)
     arrived(er, r_e)
 
     ef[...] = er[...].astype(F32).reshape(DEVICES * 16, 128)
@@ -377,11 +426,11 @@
         prod = (prod * lax.rsqrt(var + EPS)).astype(BF16)
         update = dot_tn(prod, wtri_ref[...])
         for a in range(4):
-            p = lax.rem(t, 4) * 16 + a * 4 + t // 4
+            p = lax.rem(t, 4) * 16 + lax.rem(t // 4, 2) * 8 + (a % 2 * 2 + t // 8) * 2 + a // 2
             out_p[a * 16 + t] = pm[p] + gp[p] * update[a * 32 : a * 32 + 32]
         return carry
 
-    lax.fori_loop(0, 16, final, 0)
+    lax.fori_loop(0, 16, final, 0, unroll=4)
 
     store[0].wait()
     store[1].wait()
@@ -401,8 +450,10 @@
     def _():
         arrived(lb.at[pl.ds(0, 8)], s_h)
 
-    arrived(lb.at[pl.ds(0, 56)], s_l)
-    arrived(cb.at[pl.ds(0, DEVICES - 1)], s_d)
+    arrived(lb.at[pl.ds(0, 24)], s_l)
+    arrived(lb.at[pl.ds(0, 32)], s_c)
+    for half in range(2):
+        arrived(cb.at[half, pl.ds(0, DEVICES - 1)], s_d.at[half])
     arrived(er.at[pl.ds(0, DEVICES - 1)], s_e)
 
 
@@ -442,11 +493,12 @@
             pltpu.VMEM((512, 4096), BF16),
             pltpu.VMEM((SEQ, RES, C_Z), F32),
             pltpu.VMEM((SEQ, RES, C_Z), F32),
-            pltpu.VMEM((DEVICES * 32, 128), F32),
-            pltpu.VMEM((DEVICES, 32, 128), BF16),
-            pltpu.VMEM((32, 32, 512), BF16),
+            pltpu.VMEM((2, DEVICES * 16, 128), F32),
+            pltpu.VMEM((2, DEVICES, 16, 128), BF16),
+            pltpu.VMEM((2, 32, 16, 512), BF16),
             pltpu.VMEM((512, 512), BF16),
             pltpu.VMEM((512, 512), BF16),
+            pltpu.VMEM((512, 512), F32),
             pltpu.VMEM((512, 512), BF16),
             pltpu.VMEM((64, 512), BF16),
             pltpu.VMEM((32, 16, 512), BF16),
@@ -458,8 +510,9 @@
             dma(()), dma(()),
             dma(()), dma((OWN,)),
             dma(()), dma((OWN,)),
-            dma(()), dma(()),
-            dma(()), dma(()),
+            dma(()), dma((OWN,)),
+            dma(()), dma((OWN,)),
+            dma((2,)), dma((2,)),
             dma(()), dma(()),
         ],
         compiler_params=pltpu.CompilerParams(

time: 130 us -> 105 us (0.81)
  Pallas kernels: 125 us -> 100 us
    pallas_call x1, Pallas kernels: 125 us -> 100 us  [body(): pl.pallas_call(kernel, out_shape=(jax.ShapeDtypeStruct((SEQ * RES, FEAT),...]
where the time goes in v3:
time: 105 us
  Pallas kernels  100 us (95%)
  local copies, waits for them, and re-layouts  4.22 us (4%)
    pallas_call x1, Pallas kernels, body(): pl.pallas_call(kernel, out_shape=(jax.ShapeDtypeStruct((SEQ * RES, FEAT),...  100 us
    unnamed x4, local copies, waits for them, and re-layouts  4.22 us

profile of v3, /device:TPU:1, one launch (start us, length us, event | category | flops | bytes accessed | tf_op | source)
XLA Modules:
  0.0 104.9 jit_solution(15839894272422531724)
XLA Ops:
  0.6 100.1 %shard_map.113 = (f32[2048,256]{1,0:T(8,128)}, f32[64,32,128]{2,1,0:T(8,128)}) custom-call(f32[2048,256]{1,0:T(8,128)} %bitcast.3, f32[64,32,128]{2,1,0:T(8,128)} %coup_ref.1, bf16[256,256]{1,0:T(8,128)(2,1)} %wq_ref.1, bf16[256,768]{1,0:T(8,128)(2,1)} %wx_ref.1, bf16[256,256]{1,0:T(8,128)(2,1)} %wf_ref.1, bf16[64,256]{1,0:T(8,128)(2,1)} %bitcast.5, ...), custom_call_target="tpu_custom_call" | custom-call | tf_op jit(solution)/shard_map/pallas_call | solution.py:464
  100.7 0.0 copy-start
  100.7 3.2 %copy.14 = f32[64,32,256]{2,1,0:T(8,128)} copy(f32[64,32,256]{2,1,0:T(8,128)} %bitcast.4) | data formatting | bytes 4194304
  104.0 0.0 copy-done
  104.0 1.0 copy.15
Async XLA Ops:
  100.7 3.3 %copy-start = (f32[64,32,128]{2,1,0:T(8,128)S(1)}, f32[64,32,128]{2,1,0:T(8,128)}, u32[]{:S(2)}) copy-start(f32[64,32,128]{2,1,0:T(8,128)} %get-tuple-element.9) | copy-start | bytes 3145732

commit v4 on v3

--- a/solution.py
+++ b/solution.py
@@ -43,9 +43,9 @@
 def kernel(
     x_ref, coup_ref, wq_ref, wx_ref, wf_ref, we_ref, wo_ref, wi_ref, wsw_ref, wtri_ref,
     out_m, out_p,
-    xs, nt, g, sig, sg, qs, kt, vs, ga, gt, gb, lrs, rb, lb,
+    xs, coup, nt, g, sig, sg, qs, kt, vs, ga, gt, gb, lrs, rb, lb,
     wit, wof, wbd, perm, rf, rp, om, pm, gp, cf, cb, xlr, am, bm, pa, pb, xe, es, er, ef,
-    s_x, s_a, r_a, s_sig, r_sig, s_b, r_b, s_h, r_h, s_l, r_l, s_c, r_c, s_r, r_r, s_d, r_d, s_e, r_e,
+    everyone, s_x, s_c0, s_a, r_a, s_sig, r_sig, s_b, r_b, s_h, r_h, s_t, r_t, s_l, r_l, s_c, r_c, s_r, r_r, s_d, r_d, s_e, r_e,
 ):
     r = lax.axis_index("row")
     c = lax.axis_index("col")
@@ -67,17 +67,30 @@
     ]
     load[0].start()
     load[1].start()
+    couplings = pltpu.make_async_copy(coup_ref, coup, s_c0)
 
     barrier = pltpu.get_barrier_semaphore()
 
-    def greet(d, carry):
-        peer = lax.rem(me + d, DEVICES)
+    def greet_along_row(d, carry):
         pl.semaphore_signal(
-            barrier, inc=1, device_id=(peer // COLS, lax.rem(peer, COLS)), device_id_type=MESH
+            barrier, inc=1, device_id=(lax.rem(r + d, ROWS), c), device_id_type=MESH
         )
         return carry
 
-    lax.fori_loop(1, DEVICES, greet, 0)
+    def greet_along_col(d, carry):
+        pl.semaphore_signal(
+            barrier, inc=1, device_id=(r, lax.rem(c + d, COLS)), device_id_type=MESH
+        )
+        return carry
+
+    lax.fori_loop(1, ROWS, greet_along_row, 0)
+    lax.fori_loop(1, COLS, greet_along_col, 0)
+
+    def tell(d, carry):
+        pl.semaphore_signal(
+            everyone, inc=1, device_id=(r, lax.rem(c + d, COLS)), device_id_type=MESH
+        )
+        return carry
 
     def norm_one(q, row, stats):
         n = row * OWN + q
@@ -114,9 +127,13 @@
     for q in range(OWN):
         stats = lax.fori_loop(0, ROWS, lambda row, s, q=q: norm_one(q, row, s), stats, unroll=4)
         if q == 0:
-            pl.semaphore_wait(barrier, DEVICES - 1)
+            pl.semaphore_wait(barrier, ROWS - 1 + COLS - 1)
             send_normed(0)
+            lax.fori_loop(1, COLS, tell, 0)
+        if q == 1:
+            send_normed(1)
     sig[...] = stats.astype(BF16)
+    couplings.start()
 
     wit[...] = wi_ref[...].astype(F32).T.astype(BF16)
     wof[...] = wo_ref[...].astype(F32)
@@ -137,16 +154,26 @@
 
     core = lax.rem(c, 2)
 
+    def slot(q, half):
+        return lb.at[q * 16 + core * 8 + lax.rem(c, 8) // 2 * 2 + half]
+
+    def pass_on(q, half):
+        def send_l(j, carry):
+            col = c // 8 * 8 + lax.rem(c + 2 * j, 8)
+            remote(slot(q, half), slot(q, half), s_l, r_l.at[q], r, col).start()
+            return carry
+
+        lax.fori_loop(1, 4, send_l, 0)
+
     def relay(q):
-        arrived(lb.at[pl.ds(0, 2)], r_h.at[q])
-        mine = lb.at[pl.ds(q * 16 + core * 8 + lax.rem(c, 8) // 2 * 2, 2)]
-
-        def pass_on(j, carry):
-            col = c // 8 * 8 + lax.rem(c + 2 * j, 8)
-            remote(mine, mine, s_l, r_l.at[q], r, col).start()
-            return carry
-
-        lax.fori_loop(1, 4, pass_on, 0)
+        arrived(lb.at[0], r_h.at[q])
+        mine = slot(q, c // 8)
+        remote(mine, mine, s_t, r_t.at[q], r, lax.rem(c + 8, COLS)).start()
+        pass_on(q, c // 8)
+
+    def relay_twin(q):
+        arrived(lb.at[0], r_t.at[q])
+        pass_on(q, 1 - c // 8)
 
     def send_gated(q):
         def send_b(j, carry):
@@ -165,9 +192,9 @@
     def attend(q, carry):
         arrived(g.at[q], r_a.at[q])
 
-        @pl.when(q < OWN - 1)
-        def _():
-            send_normed(q + 1)
+        @pl.when(q < OWN - 2)
+        def _():
+            send_normed(q + 2)
 
         @pl.when(q == 0)
         def _():
@@ -204,6 +231,7 @@
         @pl.when(q == 0)
         def _():
             arrived(sg, r_sig)
+            pl.semaphore_wait(everyone, COLS - 1)
 
         for part in range(2):
             rows = slice(part * 256, part * 256 + 256)
@@ -220,18 +248,16 @@
             lrs[q, :, rows] = dot_nt(we_ref[...], fresh).astype(BF16)
 
         spot = q * 16 + lax.rem(r, 2) * 8 + r // 2 * 2 + lax.rem(c, 2)
-        for half in range(2):
-            here = jnp.logical_and(rho == r, c == half * 8 + r)
-
-            @pl.when(here)
-            def _():
-                pltpu.make_async_copy(lrs.at[q, pl.ds(0, 32)], lb.at[spot], r_h.at[q]).start()
-
-            @pl.when(jnp.logical_not(here))
-            def _():
-                remote(
-                    lrs.at[q, pl.ds(0, 32)], lb.at[spot], s_h, r_h.at[q], rho, half * 8 + r
-                ).start()
+        meet = lax.rem(c, 2) * 8 + r
+        here = jnp.logical_and(rho == r, c == meet)
+
+        @pl.when(here)
+        def _():
+            pltpu.make_async_copy(lrs.at[q, pl.ds(0, 32)], lb.at[spot], r_h.at[q]).start()
+
+        @pl.when(jnp.logical_not(here))
+        def _():
+            remote(lrs.at[q, pl.ds(0, 32)], lb.at[spot], s_h, r_h.at[q], rho, meet).start()
 
         def send_r(j, carry):
             row = lax.rem(r + j, ROWS)
@@ -248,7 +274,11 @@
 
         @pl.when(q > 1)
         def _():
-            share(q - 2)
+            relay_twin(q - 2)
+
+        @pl.when(q > 2)
+        def _():
+            share(q - 3)
 
         return carry
 
@@ -262,8 +292,9 @@
 
     for q in range(OWN):
         if q == OWN - 1:
+            relay_twin(OWN - 2)
             relay(OWN - 1)
-            share(OWN - 2)
+            share(OWN - 3)
         arrived(rb.at[pl.ds(0, ROWS)], r_r.at[q])
         lax.fori_loop(0, ROWS, by_channel, q, unroll=2)
     for k in range(4):
@@ -292,7 +323,7 @@
                 e, q = f % 4, b * 2 + f // 4
                 i = a % 2 * 32 + (e % 2 * 4 + a // 2 * 2 + e // 2) * 4 + q
                 pm[q * 16 + e * 4 + a] = (
-                    coup_ref[i] + update[f * 32 : f * 32 + 32, a * 128 : a * 128 + 128]
+                    coup[i] + update[f * 32 : f * 32 + 32, a * 128 : a * 128 + 128]
                 )
 
     def entry(b, carry):
@@ -318,8 +349,9 @@
         for q in (half * 2, half * 2 + 1):
             arrived(lb.at[pl.ds(0, 8)], r_c.at[q])
             lax.fori_loop(q * 2, q * 2 + 2, outer, 0)
-            if q == OWN - 2:
-                share(OWN - 1)
+            if q == 0:
+                relay_twin(OWN - 1)
+                share(OWN - 2)
         mid(half)
         lax.fori_loop(half * 4, half * 4 + 4, entry, 0)
 
@@ -339,7 +371,9 @@
             cb.at[half, me], xlr.at[half, corner, :, pl.ds(lanes_at, 128)], r_d.at[half]
         ).start()
 
+    couplings.wait()
     pairs(0)
+    share(OWN - 1)
     deal_out(0)
     pairs(1)
     deal_out(1)
@@ -440,21 +474,37 @@
     arrived(gb.at[pl.ds(0, 28)], s_b)
     arrived(rb.at[pl.ds(0, 28)], s_r)
 
-    relays_itself = jnp.logical_and(rho == r, lax.rem(c, 8) == r)
-
-    @pl.when(relays_itself)
+
+    @pl.when(jnp.logical_not(jnp.logical_and(rho == r, lax.rem(c, 2) * 8 + r == c)))
     def _():
-        arrived(lb.at[pl.ds(0, 4)], s_h)
-
-    @pl.when(jnp.logical_not(relays_itself))
-    def _():
-        arrived(lb.at[pl.ds(0, 8)], s_h)
-
+        arrived(lb.at[pl.ds(0, OWN)], s_h)
+
+    arrived(lb.at[pl.ds(0, OWN)], s_t)
     arrived(lb.at[pl.ds(0, 24)], s_l)
     arrived(lb.at[pl.ds(0, 32)], s_c)
     for half in range(2):
         arrived(cb.at[half, pl.ds(0, DEVICES - 1)], s_d.at[half])
     arrived(er.at[pl.ds(0, DEVICES - 1)], s_e)
+
+
+def hand_over(m_ref, p_ref, out_m, out_p, m, p, sems):
+    def pieces(source, held, result, count, first):
+        rows = held.shape[0] // count
+        for k in range(count):
+            at = pl.ds(k * rows, rows)
+            yield (
+                pltpu.make_async_copy(source.at[at], held.at[at], sems.at[first + k]),
+                pltpu.make_async_copy(held.at[at], result.at[at], sems.at[first + k]),
+            )
+
+    copies = list(pieces(m_ref, m, out_m, 8, 0)) + list(pieces(p_ref, p, out_p, 4, 8))
+    for load, _ in copies:
+        load.start()
+    for load, store in copies:
+        load.wait()
+        store.start()
+    for _, store in copies:
+        store.wait()
 
 
 def body(x, coup, wq, wx, wf, we, wo, wi, wsw, wtri):
@@ -467,10 +517,11 @@
             jax.ShapeDtypeStruct((SEQ * RES, FEAT), F32),
             jax.ShapeDtypeStruct((SEQ, RES, C_Z), F32),
         ),
-        in_specs=[hbm] + [vmem] * 9,
+        in_specs=[hbm] * 2 + [vmem] * 8,
         out_specs=(hbm, vmem),
         scratch_shapes=[
             pltpu.VMEM((2, SEQ * RES, 128), F32),
+            pltpu.VMEM((SEQ, RES, C_Z), F32),
             pltpu.VMEM((OWN, ROWS, SEQ, FEAT), BF16),
             pltpu.VMEM((OWN, ROWS, SEQ, FEAT), BF16),
             pltpu.VMEM((SEQ, 128), BF16),
@@ -504,10 +555,13 @@
             pltpu.VMEM((32, 16, 512), BF16),
             pltpu.VMEM((DEVICES, 16, 128), BF16),
             pltpu.VMEM((DEVICES * 16, 128), F32),
+            pltpu.SemaphoreType.REGULAR,
             dma((2,)),
+            dma(()),
             dma((OWN,)), dma((OWN,)),
             dma(()), dma(()),
             dma(()), dma(()),
+            dma(()), dma((OWN,)),
             dma(()), dma((OWN,)),
             dma(()), dma((OWN,)),
             dma(()), dma((OWN,)),
@@ -519,6 +573,18 @@
             collective_id=0, has_side_effects=True, vmem_limit_bytes=56 * 2**20
         ),
     )(x.reshape(SEQ * RES, FEAT), coup, wq, wx, wf, we.T, wo, wi, wsw, wtri)
+    out_m, out_p = pl.pallas_call(
+        hand_over,
+        out_shape=(
+            jax.ShapeDtypeStruct((SEQ * RES, FEAT), F32),
+            jax.ShapeDtypeStruct((SEQ, RES, C_Z), F32),
+        ),
+        in_specs=[hbm] * 2,
+        out_specs=(hbm, hbm),
+        scratch_shapes=[
+            pltpu.VMEM((SEQ * RES, FEAT), F32), pltpu.VMEM((SEQ, RES, C_Z), F32), dma((12,)),
+        ],
+    )(out_m, out_p)
     return out_m.reshape(SEQ, RES, FEAT), out_p
 
 

time: 105 us -> 97.4 us (0.928)
  local copies, waits for them, and re-layouts: 4.22 us -> 0 us
  Pallas kernels: 100 us -> 96.6 us
    pallas_call x1, Pallas kernels: 100 us -> 93.9 us  [body(): pl.pallas_call(kernel, out_shape=(jax.ShapeDtypeStruct((SEQ * RES, FEAT),...]
    unnamed x4 -> x0, local copies, waits for them, and re-layouts: 4.22 us -> none
    pallas_call x0 -> x1, Pallas kernels: none -> 2.7 us  [body(): pl.pallas_call(hand_over, out_shape=(jax.ShapeDtypeStruct((SEQ * RES, FEA...]
where the time goes in v4:
time: 97.4 us; the launch traced here: 97.2 us
  Pallas kernels  96.6 us (99%)
    pallas_call x1, Pallas kernels, body(): pl.pallas_call(kernel, out_shape=(jax.ShapeDtypeStruct((SEQ * RES, FEAT),...  93.9 us
    pallas_call x1, Pallas kernels, body(): pl.pallas_call(hand_over, out_shape=(jax.ShapeDtypeStruct((SEQ * RES, FEA...  2.7 us

profile of v4, /device:TPU:1, one launch (start us, length us, event | category | flops | bytes accessed | tf_op | source)
XLA Modules:
  0.0 97.2 jit_solution(6077371863108838254)
XLA Ops:
  0.6 93.9 %shard_map.113 = (f32[2048,256]{1,0:T(8,128)}, f32[64,32,128]{2,1,0:T(8,128)}) custom-call(f32[2048,256]{1,0:T(8,128)} %bitcast.3, f32[64,32,128]{2,1,0:T(8,128)} %coup_ref.1, bf16[256,256]{1,0:T(8,128)(2,1)} %wq_ref.1, bf16[256,768]{1,0:T(8,128)(2,1)} %wx_ref.1, bf16[256,256]{1,0:T(8,128)(2,1)} %wf_ref.1, bf16[64,256]{1,0:T(8,128)(2,1)} %bitcast.4, ...), custom_call_target="tpu_custom_call" | custom-call | tf_op jit(solution)/shard_map/pallas_call | solution.py:514
  94.5 2.7 %shard_map.114 = (f32[2048,256]{1,0:T(8,128)}, f32[64,32,128]{2,1,0:T(8,128)}) custom-call(f32[2048,256]{1,0:T(8,128)} %get-tuple-element.6.m_ref, f32[64,32,128]{2,1,0:T(8,128)} %get-tuple-element.7.p_ref), custom_call_target="tpu_custom_call" | custom-call | tf_op jit(solution)/shard_map/pallas_call | solution.py:576

commit v5 on v4

--- a/solution.py
+++ b/solution.py
@@ -41,11 +41,12 @@
 
 
 def kernel(
-    x_ref, coup_ref, wq_ref, wx_ref, wf_ref, we_ref, wo_ref, wi_ref, wsw_ref, wtri_ref,
+    x_ref, coup_ref, wq_in, wx_in, wf_in, we_in, wo_in, wi_in, wsw_in, wtri_in,
     out_m, out_p,
+    wq_ref, wx_ref, wf_ref, we_ref, wo_ref, wi_ref, wsw_ref, wtri_ref,
     xs, coup, nt, g, sig, sg, qs, kt, vs, ga, gt, gb, lrs, rb, lb,
     wit, wof, wbd, perm, rf, rp, om, pm, gp, cf, cb, xlr, am, bm, pa, pb, xe, es, er, ef,
-    everyone, s_x, s_c0, s_a, r_a, s_sig, r_sig, s_b, r_b, s_h, r_h, s_t, r_t, s_l, r_l, s_c, r_c, s_r, r_r, s_d, r_d, s_e, r_e,
+    everyone, s_x, s_c0, s_w, s_o, s_a, r_a, s_sig, r_sig, s_b, r_b, s_h, r_h, s_t, r_t, s_l, r_l, s_c, r_c, s_r, r_r, s_d, r_d, s_e, r_e,
 ):
     r = lax.axis_index("row")
     c = lax.axis_index("col")
@@ -68,6 +69,15 @@
     load[0].start()
     load[1].start()
     couplings = pltpu.make_async_copy(coup_ref, coup, s_c0)
+    weights_in = [
+        pltpu.make_async_copy(source, held, s_w.at[k])
+        for k, (source, held) in enumerate(
+            (
+                (wq_in, wq_ref), (wx_in, wx_ref), (wf_in, wf_ref), (we_in, we_ref),
+                (wo_in, wo_ref), (wi_in, wi_ref), (wsw_in, wsw_ref), (wtri_in, wtri_ref),
+            )
+        )
+    ]
 
     barrier = pltpu.get_barrier_semaphore()
 
@@ -107,6 +117,8 @@
         stats = jnp.where(lane(128) == n, high, stats)
         return jnp.where(lane(128) == n + RES, sd - high, stats)
 
+    for copy in weights_in:
+        copy.start()
     load[0].wait()
     load[1].wait()
     def send_normed(q):
@@ -134,6 +146,8 @@
             send_normed(1)
     sig[...] = stats.astype(BF16)
     couplings.start()
+    for copy in weights_in:
+        copy.wait()
 
     wit[...] = wi_ref[...].astype(F32).T.astype(BF16)
     wof[...] = wo_ref[...].astype(F32)
@@ -461,11 +475,14 @@
         update = dot_tn(prod, wtri_ref[...])
         for a in range(4):
             p = lax.rem(t, 4) * 16 + lax.rem(t // 4, 2) * 8 + (a % 2 * 2 + t // 8) * 2 + a // 2
-            out_p[a * 16 + t] = pm[p] + gp[p] * update[a * 32 : a * 32 + 32]
+            i = a * 16 + t
+            coup[i] = pm[p] + gp[p] * update[a * 32 : a * 32 + 32]
+            pltpu.make_async_copy(coup.at[i], out_p.at[i], s_o).start()
         return carry
 
     lax.fori_loop(0, 16, final, 0, unroll=4)
 
+    pltpu.make_async_copy(coup, out_p, s_o).wait()
     store[0].wait()
     store[1].wait()
     for q in range(OWN):
@@ -508,7 +525,7 @@
 
 
 def body(x, coup, wq, wx, wf, we, wo, wi, wsw, wtri):
-    vmem = pl.BlockSpec(memory_space=pltpu.VMEM)
+    weights = (wq, wx, wf, we.T, wo, wi, wsw, wtri)
     hbm = pl.BlockSpec(memory_space=pl.ANY)
     dma = pltpu.SemaphoreType.DMA
     out_m, out_p = pl.pallas_call(
@@ -517,9 +534,10 @@
             jax.ShapeDtypeStruct((SEQ * RES, FEAT), F32),
             jax.ShapeDtypeStruct((SEQ, RES, C_Z), F32),
         ),
-        in_specs=[hbm] * 2 + [vmem] * 8,
-        out_specs=(hbm, vmem),
-        scratch_shapes=[
+        in_specs=[hbm] * 10,
+        out_specs=(hbm, hbm),
+        scratch_shapes=[pltpu.VMEM(w.shape, BF16) for w in weights]
+        + [
             pltpu.VMEM((2, SEQ * RES, 128), F32),
             pltpu.VMEM((SEQ, RES, C_Z), F32),
             pltpu.VMEM((OWN, ROWS, SEQ, FEAT), BF16),
@@ -558,6 +576,8 @@
             pltpu.SemaphoreType.REGULAR,
             dma((2,)),
             dma(()),
+            dma((8,)),
+            dma(()),
             dma((OWN,)), dma((OWN,)),
             dma(()), dma(()),
             dma(()), dma(()),
@@ -572,7 +592,7 @@
         compiler_params=pltpu.CompilerParams(
             collective_id=0, has_side_effects=True, vmem_limit_bytes=56 * 2**20
         ),
-    )(x.reshape(SEQ * RES, FEAT), coup, wq, wx, wf, we.T, wo, wi, wsw, wtri)
+    )(x.reshape(SEQ * RES, FEAT), coup, *weights)
     out_m, out_p = pl.pallas_call(
         hand_over,
         out_shape=(

time: 97.4 us -> 96.1 us (0.987)
  Pallas kernels: 96.6 us -> 95.3 us
    pallas_call x1, Pallas kernels: 93.9 us -> 92.6 us  [body(): pl.pallas_call(kernel, out_shape=(jax.ShapeDtypeStruct((SEQ * RES, FEAT),...]
where the time goes in v5:
time: 96.1 us; the launch traced here: 95.9 us
  Pallas kernels  95.3 us (99%)
    pallas_call x1, Pallas kernels, body(): pl.pallas_call(kernel, out_shape=(jax.ShapeDtypeStruct((SEQ * RES, FEAT),...  92.6 us
    pallas_call x1, Pallas kernels, body(): pl.pallas_call(hand_over, out_shape=(jax.ShapeDtypeStruct((SEQ * RES, FEA...  2.7 us

profile of v5, /device:TPU:1, one launch (start us, length us, event | category | flops | bytes accessed | tf_op | source)
XLA Modules:
  0.0 95.9 jit_solution(15417158213372028271)
XLA Ops:
  0.6 92.6 %shard_map.113 = (f32[2048,256]{1,0:T(8,128)}, f32[64,32,128]{2,1,0:T(8,128)}) custom-call(f32[2048,256]{1,0:T(8,128)} %bitcast.3, f32[64,32,128]{2,1,0:T(8,128)} %coup_ref.1, bf16[256,256]{1,0:T(8,128)(2,1)} %wq_in.1, bf16[256,768]{1,0:T(8,128)(2,1)} %wx_in.1, bf16[256,256]{1,0:T(8,128)(2,1)} %wf_in.1, bf16[64,256]{1,0:T(8,128)(2,1)} %bitcast.4, ...), custom_call_target="tpu_custom_call" | custom-call | tf_op jit(solution)/shard_map/pallas_call | solution.py:531
  93.2 2.7 %shard_map.114 = (f32[2048,256]{1,0:T(8,128)}, f32[64,32,128]{2,1,0:T(8,128)}) custom-call(f32[2048,256]{1,0:T(8,128)} %get-tuple-element.6.m_ref, f32[64,32,128]{2,1,0:T(8,128)} %get-tuple-element.7.p_ref), custom_call_target="tpu_custom_call" | custom-call | tf_op jit(solution)/shard_map/pallas_call | solution.py:596

commit v6 on v5

--- a/solution.py
+++ b/solution.py
@@ -63,7 +63,7 @@
         pltpu.make_async_copy(ref, ref, sem).wait()
 
     load = [
-        pltpu.make_async_copy(x_ref.at[:, pl.ds(k * 128, 128)], xs.at[k], s_x.at[k])
+        pltpu.make_async_copy(x_ref.at[:, pl.ds(k * 128, 128)], xs.at[k, pl.ds(0, SEQ * RES)], s_x.at[k])
         for k in range(2)
     ]
     load[0].start()
@@ -150,7 +150,7 @@
         copy.wait()
 
     wit[...] = wi_ref[...].astype(F32).T.astype(BF16)
-    wof[...] = wo_ref[...].astype(F32)
+    wof[0:1024] = wo_ref[...].astype(F32)
     wbd[...] = jnp.zeros(wbd.shape, BF16)
 
     def spread(d, carry):
@@ -312,7 +312,7 @@
         arrived(rb.at[pl.ds(0, ROWS)], r_r.at[q])
         lax.fori_loop(0, ROWS, by_channel, q, unroll=2)
     for k in range(4):
-        rp[:, k * 128 : k * 128 + 128] = rf[k].astype(BF16)
+        rp[:, k * 128 : k * 128 + 128] = rf[k, 0:1024].astype(BF16)
 
     for q in range(OWN):
         send_gated(q)
@@ -370,7 +370,7 @@
         lax.fori_loop(half * 4, half * 4 + 4, entry, 0)
 
     def deal_out(half):
-        cb[half] = cf[half].astype(BF16).reshape(DEVICES, 16, 128)
+        cb[half] = cf[half, 0 : DEVICES * 16].astype(BF16).reshape(DEVICES, 16, 128)
 
         def send_d(d, carry):
             peer = lax.rem(me + d, DEVICES)
@@ -406,7 +406,7 @@
 
     lax.fori_loop(0, RES // 4, refresh, 0)
     store = [
-        pltpu.make_async_copy(xs.at[k], out_m.at[:, pl.ds(k * 128, 128)], s_x.at[k])
+        pltpu.make_async_copy(xs.at[k, pl.ds(0, SEQ * RES)], out_m.at[:, pl.ds(k * 128, 128)], s_x.at[k])
         for k in range(2)
     ]
     store[0].start()
@@ -465,7 +465,7 @@
     lax.fori_loop(0, ROWS, deal, 0)
     arrived(er, r_e)
 
-    ef[...] = er[...].astype(F32).reshape(DEVICES * 16, 128)
+    ef[0 : DEVICES * 16] = er[...].astype(F32).reshape(DEVICES * 16, 128)
 
     def final(t, carry):
         prod = ef[pl.ds(t, DEVICES, stride=16), :]
@@ -538,7 +538,7 @@
         out_specs=(hbm, hbm),
         scratch_shapes=[pltpu.VMEM(w.shape, BF16) for w in weights]
         + [
-            pltpu.VMEM((2, SEQ * RES, 128), F32),
+            pltpu.VMEM((2, SEQ * RES + RES, 128), F32),
             pltpu.VMEM((SEQ, RES, C_Z), F32),
             pltpu.VMEM((OWN, ROWS, SEQ, FEAT), BF16),
             pltpu.VMEM((OWN, ROWS, SEQ, FEAT), BF16),
@@ -554,15 +554,15 @@
             pltpu.VMEM((RES, 32, ALL), BF16),
             pltpu.VMEM((SEQ, 32, ALL), BF16),
             pltpu.VMEM((512, C_Z), BF16),
-            pltpu.VMEM((1024, C_Z), F32),
+            pltpu.VMEM((1024 + 32, C_Z), F32),
             pltpu.VMEM((4096, 512), BF16),
             pltpu.VMEM((512, 512), BF16),
-            pltpu.VMEM((4, 1024, 128), F32),
+            pltpu.VMEM((4, 1024 + 32, 128), F32),
             pltpu.VMEM((1024, ALL), BF16),
             pltpu.VMEM((512, 4096), BF16),
             pltpu.VMEM((SEQ, RES, C_Z), F32),
             pltpu.VMEM((SEQ, RES, C_Z), F32),
-            pltpu.VMEM((2, DEVICES * 16, 128), F32),
+            pltpu.VMEM((2, DEVICES * 16 + 16, 128), F32),
             pltpu.VMEM((2, DEVICES, 16, 128), BF16),
             pltpu.VMEM((2, 32, 16, 512), BF16),
             pltpu.VMEM((512, 512), BF16),
@@ -572,7 +572,7 @@
             pltpu.VMEM((64, 512), BF16),
             pltpu.VMEM((32, 16, 512), BF16),
             pltpu.VMEM((DEVICES, 16, 128), BF16),
-            pltpu.VMEM((DEVICES * 16, 128), F32),
+            pltpu.VMEM((DEVICES * 16 + 16, 128), F32),
             pltpu.SemaphoreType.REGULAR,
             dma((2,)),
             dma(()),

time: 96.1 us -> 96.1 us (level)
  no operation moved by 1% of the time
where the time goes in v6:
time: 96.1 us; the launch traced here: 95.9 us
  Pallas kernels  95.3 us (99%)
    pallas_call x1, Pallas kernels, body(): pl.pallas_call(kernel, out_shape=(jax.ShapeDtypeStruct((SEQ * RES, FEAT),...  92.6 us
    pallas_call x1, Pallas kernels, body(): pl.pallas_call(hand_over, out_shape=(jax.ShapeDtypeStruct((SEQ * RES, FEA...  2.7 us

profile of v6, /device:TPU:1, one launch (start us, length us, event | category | flops | bytes accessed | tf_op | source)
XLA Modules:
  0.0 95.9 jit_solution(16817365798210514629)
XLA Ops:
  0.6 92.6 %shard_map.113 = (f32[2048,256]{1,0:T(8,128)}, f32[64,32,128]{2,1,0:T(8,128)}) custom-call(f32[2048,256]{1,0:T(8,128)} %bitcast.3, f32[64,32,128]{2,1,0:T(8,128)} %coup_ref.1, bf16[256,256]{1,0:T(8,128)(2,1)} %wq_in.1, bf16[256,768]{1,0:T(8,128)(2,1)} %wx_in.1, bf16[256,256]{1,0:T(8,128)(2,1)} %wf_in.1, bf16[64,256]{1,0:T(8,128)(2,1)} %bitcast.4, ...), custom_call_target="tpu_custom_call" | custom-call | tf_op jit(solution)/shard_map/pallas_call | solution.py:531
  93.2 2.7 %shard_map.114 = (f32[2048,256]{1,0:T(8,128)}, f32[64,32,128]{2,1,0:T(8,128)}) custom-call(f32[2048,256]{1,0:T(8,128)} %get-tuple-element.6.m_ref, f32[64,32,128]{2,1,0:T(8,128)} %get-tuple-element.7.p_ref), custom_call_target="tpu_custom_call" | custom-call | tf_op jit(solution)/shard_map/pallas_call | solution.py:596
